TPU v7x, 32 devices: a whole 2x2x4 slice. The times are simulated.
32 devices in a mesh: narrow: 4 (over x, core), wide: 8 (over z, y).
Axes of the slice: x: 2, y: 2, z: 4, core: 2. Of those that a mesh axis runs over, the one named last changes fastest.
Arguments:
- tokens: bfloat16 [12288, 512], P(('narrow', 'wide')), may hold values from -6 to 6
- gain_one: float32 [512], replicated, may hold values from 0.5 to 1.5
- shift_one: float32 [512], replicated, may hold values from -1.25 to 1.25
- query_w: bfloat16 [512, 512], replicated, may hold values from -0.25 to 0.25
- key_w: bfloat16 [512, 512], replicated, may hold values from -0.25 to 0.25
- value_w: bfloat16 [512, 512], replicated, may hold values from -0.25 to 0.25
- out_w: bfloat16 [512, 512], replicated, may hold values from -1.5 to 1.5
- gain_two: float32 [512], replicated, may hold values from 0.5 to 1.5
- shift_two: float32 [512], replicated, may hold values from -1.25 to 1.25
- router_w: bfloat16 [512, 8], replicated, may hold values from -0.1875 to 0.1875
- up_w: bfloat16 [8, 512, 2048], P('wide'), may hold values from -0.25 to 0.25
- up_bias: float32 [8, 2048], P('wide'), may hold values from -0.625 to 0.625
- down_w: bfloat16 [8, 2048, 512], P('wide'), may hold values from -4 to 4
- down_bias: float32 [8, 512], P('wide'), may hold values from -12 to 12
- picks: int32 [12288, 2], P(('narrow', 'wide')), may hold values from 0 to 7, all different within a row
- ranks: int32 [12288, 2], P(('narrow', 'wide')), may hold values from 0 to 767, as said below
- out_grad: bfloat16 [12288, 512], P(('narrow', 'wide')), may hold values from -6 to 6
Outputs:
- block_out: bfloat16 [12288, 512], P(('narrow', 'wide'))
- tokens_grad: bfloat16 [12288, 512], P(('narrow', 'wide'))
- gain_one_grad: float32 [512], replicated
- shift_one_grad: float32 [512], replicated
- query_grad: float32 [512, 512], replicated
- key_grad: float32 [512, 512], replicated
- value_grad: float32 [512, 512], replicated
- out_w_grad: float32 [512, 512], replicated
- gain_two_grad: float32 [512], replicated
- shift_two_grad: float32 [512], replicated
- router_grad: float32 [512, 8], replicated
- up_grad: float32 [8, 512, 2048], P('wide')
- up_bias_grad: float32 [8, 2048], P('wide')
- down_grad: float32 [8, 2048, 512], P('wide')
- down_bias_grad: float32 [8, 512], P('wide')
- expert_counts: int32 [8, 2], replicated
Inputs may be any that keep to these rules, and one draw needn't show every extreme that they name: `picks`: the two experts of a row differ. `ranks`: within the 384 tokens of each device block, the 768 entries are all different; a smaller rank takes its slot first.
All inputs are finite; a program needn't handle non-finite values.
Results may differ from a plain program's by a relative error of at most 0.017.
Values may be sent and summed in bfloat16 or wider, within the bound.
No kernel may reach another device: no remote copies, remote signals or barrier semaphores. Data moves between devices by JAX's collectives and lax.ppermute only.
A program may use at most 128 MiB of HBM per device.

v0:
```python
import functools
import math

import jax
import jax.numpy as jnp
from jax import lax
from jax.experimental import pallas as pl
from jax.experimental.pallas import tpu as pltpu
from jax.sharding import PartitionSpec as P

HEADS = 8
PATCHES = 48
EPSILON = 1e-06
LANES = 128
MIB = 1 << 20
F32 = jnp.float32
BF16 = jnp.bfloat16

VMEM = functools.partial(pl.BlockSpec, memory_space=pltpu.VMEM)
SMEM = functools.partial(pl.BlockSpec, memory_space=pltpu.SMEM)


def shape(dims, dtype):
    return jax.ShapeDtypeStruct(dims, dtype)


def dot(a, b):
    return jnp.dot(a, b, preferred_element_type=F32)


def dot_nt(a, b):
    return lax.dot_general(a, b, (((1,), (1,)), ((), ())), preferred_element_type=F32)


def dot_tn(a, b):
    return lax.dot_general(a, b, (((0,), (0,)), ((), ())), preferred_element_type=F32)


def params(mib):
    return pltpu.CompilerParams(vmem_limit_bytes=mib * MIB)


def cost(us):
    return pl.CostEstimate(flops=int(us * 1.0e9), bytes_accessed=int(us * 1.0e5), transcendentals=0)


class Held:
    def __init__(self, value):
        self.value = value
        self.shape, self.dtype, self.ndim = value.shape, value.dtype, value.ndim


def placed(value):
    if isinstance(value, Held):
        return value.value
    if isinstance(value, Part):
        value = value.value
    return value if value.ndim == 1 else pltpu.with_memory_space_constraint(value, pltpu.HBM)


def whole_spec(dims):
    return pl.BlockSpec(tuple(dims), lambda *_: (0,) * len(dims))


def held(dims, dtype):
    return pltpu.VMEM(tuple(dims), dtype)


def far(dims, dtype):
    return pltpu.HBM(tuple(dims), dtype)


def loose(value):
    return pl.BlockSpec(memory_space=pl.ANY if isinstance(value, Held) else pltpu.HBM)


def run(kernel, args, outs, mib, us, name, scratch=(), after=(), grid=(1,), in_specs=None, out_specs=None, free=False, **more):
    given = len(args)
    if in_specs is None:
        in_specs = [SMEM() if a.ndim == 1 else whole_spec(a.shape) for a in args]
    if out_specs is None:
        out_specs = [whole_spec(o.shape) for o in outs]

    def body(*refs):
        kernel(*refs[:given], *refs[given + len(after) :])

    return pl.pallas_call(
        body,
        grid=grid,
        in_specs=list(in_specs) + [loose(value) for value in after],
        out_specs=tuple(out_specs),
        out_shape=tuple(shape(o.shape, o.dtype) if free else far(o.shape, o.dtype) for o in outs),
        scratch_shapes=list(scratch),
        compiler_params=params(mib),
        cost_estimate=cost(us),
        name=name,
        **more,
    )(*map(placed, args), *map(placed, after))


class Part:
    def __init__(self, value, tile, at, rows=False):
        some, all_of = slice(at * tile, (at + 1) * tile), slice(None)
        self.value, self.index = value, (some, all_of) if rows else (all_of, some)
        self.shape = (tile, value.shape[1]) if rows else (value.shape[0], tile)
        self.dtype, self.ndim = value.dtype, 2


class Arriving:
    def __init__(self, source, target, semaphore):
        self.target, self.shape = target, target.shape
        self.copy = pltpu.make_async_copy(source, target, semaphore)
        self.copy.start()
        self.here = False

    def wait(self):
        if not self.here:
            self.copy.wait()
            self.here = True

    def __getitem__(self, index):
        self.wait()
        return self.target[index]


class Leaving:
    def __init__(self, source, target, semaphores):
        self.source, self.target, self.semaphores = source, target, semaphores
        self.shape = source.shape
        self.copies = []

    def __getitem__(self, index):
        return self.source[index]

    def __setitem__(self, index, value):
        self.source[index] = value

    def flush(self, *index):
        one, two = (self.source.at[index], self.target.at[index]) if index else (self.source, self.target)
        self.copies.append(pltpu.make_async_copy(one, two, self.semaphores.at[len(self.copies)]))
        self.copies[-1].start()

    def wait(self):
        for copy in self.copies:
            copy.wait()


def fuse(kernel, args, outs, mib, us, name, scratch=(), after=()):
    is_far = [not isinstance(a, Held) and a.ndim > 1 for a in args]
    out_far = [o.memory_space == pltpu.HBM for o in outs]
    given, made = len(args), len(outs)

    def body(*refs):
        ins, refs = list(refs[:given]), refs[given + len(after) :]
        results, refs = list(refs[:made]), list(refs[made:])
        arrivals, departures = refs.pop(), refs.pop()
        coming, going = [], []
        for at in range(given):
            if is_far[at]:
                source = ins[at].at[args[at].index] if isinstance(args[at], Part) else ins[at]
                ins[at] = Arriving(source, refs.pop(0), arrivals.at[len(coming)])
                coming.append(ins[at])
        for at in range(made):
            if out_far[at]:
                results[at] = Leaving(refs.pop(0), results[at], departures.at[len(going)])
                going.append(results[at])
        kernel(*ins, *results, *refs)
        for item in coming + going:
            item.wait()

    def spec(value):
        if isinstance(value, Held):
            return VMEM()
        return SMEM() if value.ndim == 1 else pl.BlockSpec(memory_space=pltpu.HBM)

    return pl.pallas_call(
        body,
        in_specs=[spec(a) for a in args] + [loose(value) for value in after],
        out_specs=tuple(pl.BlockSpec(memory_space=o.memory_space) for o in outs),
        out_shape=tuple(outs),
        scratch_shapes=[pltpu.VMEM(a.shape, a.dtype) for a, there in zip(args, is_far) if there]
        + [pltpu.VMEM(o.shape, o.dtype) for o, there in zip(outs, out_far) if there]
        + list(scratch)
        + [pltpu.SemaphoreType.DMA((max(sum(out_far), 1), 8)), pltpu.SemaphoreType.DMA((max(sum(is_far), 1),))],
        compiler_params=params(mib),
        cost_estimate=cost(us),
        name=name,
    )(*map(placed, args), *map(placed, after))


def norm_rows(values):
    center = values - jnp.mean(values, axis=-1, keepdims=True)
    spread = jnp.mean(center * center, axis=-1, keepdims=True)
    rate = lax.rsqrt(spread + EPSILON)
    return center * rate, rate


def norm_back(hat, rate, gain, grad):
    scaled = grad * gain
    mean_one = jnp.mean(scaled, axis=-1, keepdims=True)
    mean_two = jnp.mean(scaled * hat, axis=-1, keepdims=True)
    return rate * (scaled - mean_one - hat * mean_two)


def route(capacity, experts, picks_ref, ranks_ref, spread_ref, target_ref, count_ref):
    count = picks_ref.shape[1]
    slots_all = experts * capacity
    span = 1 << (2 * count - 1).bit_length()
    picks = picks_ref[...].astype(F32)
    base = picks * span
    order = base + ranks_ref[...].astype(F32)
    padded = jnp.concatenate([picks, order, jnp.zeros((4, count), F32)], axis=0)
    turned = jnp.transpose(padded)
    targets = []
    for j in range(2):
        row = order[j : j + 1]
        floor = base[j : j + 1]
        slot = jnp.zeros((1, count), F32)
        for other in range(2):
            column = turned[:, 2 + other : 3 + other]
            ahead = (column < row) & (column >= floor)
            slot = slot + jnp.sum(jnp.where(ahead, 1.0, 0.0), axis=0, keepdims=True)
        kept = slot < capacity
        targets.append(jnp.where(kept, picks[j : j + 1] * capacity + slot, float(slots_all)))
    target_turned = jnp.transpose(jnp.concatenate(targets + [jnp.zeros((6, count), F32)], axis=0))
    target_ref[...] = target_turned
    lane = lax.broadcasted_iota(jnp.int32, (count, LANES), 1).astype(F32)
    kept_count = jnp.zeros((1, LANES), F32)
    all_count = jnp.zeros((1, LANES), F32)
    for j in range(2):
        named = jnp.where(turned[:, j : j + 1] == lane, 1.0, 0.0)
        live = jnp.where(target_turned[:, j : j + 1] < slots_all, 1.0, 0.0)
        all_count = all_count + jnp.sum(named, axis=0, keepdims=True)
        kept_count = kept_count + jnp.sum(named * live, axis=0, keepdims=True)
    count_ref[...] = jnp.concatenate([kept_count, all_count - kept_count, jnp.zeros((6, LANES), F32)], axis=0)
    step = 64
    for start in range(0, slots_all, step):
        index = lax.broadcasted_iota(jnp.int32, (step, count), 0).astype(F32) + float(start)
        hit = (index == targets[0]) | (index == targets[1])
        spread_ref[start : start + step, :] = jnp.where(hit, 1.0, 0.0).astype(BF16)


def head_masks(width):
    lane = lax.broadcasted_iota(jnp.int32, (1, width), 1)
    return lane < width // 2


def stack_heads(pair, low):
    zero = jnp.zeros_like(pair)
    return jnp.concatenate([jnp.where(low, pair, zero), jnp.where(low, zero, pair)], axis=0)


def attention_kernel(
    capacity,
    experts,
    tokens_ref,
    gain_one_ref,
    shift_one_ref,
    picks_ref,
    ranks_ref,
    query_w_ref,
    key_w_ref,
    value_w_ref,
    out_w_ref,
    gain_two_ref,
    shift_two_ref,
    spread_ref,
    target_ref,
    count_ref,
    resid_ref,
    normed_ref,
    query_ref,
    key_ref,
    value_ref,
    weight_ref,
    mixed_ref,
    sent_ref,
):
    count, width = tokens_ref.shape
    inputs = tokens_ref[...].astype(F32)
    hat, _ = norm_rows(inputs)
    normed_ref[...] = (hat * gain_one_ref[...] + shift_one_ref[...]).astype(BF16)
    normed_ref.flush()
    route(capacity, experts, picks_ref, ranks_ref, spread_ref, target_ref, count_ref)
    spread_ref.flush()
    target_ref.flush()
    count_ref.flush()
    normed = normed_ref[...]
    scale = 1.0 / math.sqrt(width // HEADS)
    query_ref[...] = (dot(normed, query_w_ref[...]).astype(BF16).astype(F32) * scale).astype(BF16)
    query_ref.flush()
    key_ref[...] = dot(normed, key_w_ref[...]).astype(BF16)
    key_ref.flush()
    value_ref[...] = dot(normed, value_w_ref[...]).astype(BF16)
    value_ref.flush()
    pairs = HEADS // 2
    wide = width // pairs
    block = 2 * PATCHES
    low = head_masks(wide)
    row_image = (lax.broadcasted_iota(jnp.int32, (2 * block, block), 0) % block) // PATCHES
    column_image = lax.broadcasted_iota(jnp.int32, (2 * block, block), 1) // PATCHES
    bias = jnp.where(row_image == column_image, 0.0, -1e30)
    together = 8
    cells = [(item, pair) for item in range(count // block) for pair in range(pairs)]
    for start in range(0, len(cells), together):
        work = []
        for item, pair in cells[start : start + together]:
            rows = slice(item * block, (item + 1) * block)
            lanes = slice(pair * wide, (pair + 1) * wide)
            scores = dot_nt(stack_heads(query_ref[rows, lanes], low), key_ref[rows, lanes]) + bias
            work.append((rows, lanes, scores))
        tops = [jnp.max(scores, axis=-1, keepdims=True) for _, _, scores in work]
        powers = [jnp.exp(scores - top) for (_, _, scores), top in zip(work, tops)]
        totals = [jnp.sum(power, axis=-1, keepdims=True) for power in powers]
        lows = [(power / total).astype(BF16) for power, total in zip(powers, totals)]
        for (item, pair), weights in zip(cells[start : start + together], lows):
            weight_ref[item, pair] = weights
        for (rows, lanes, _), weights in zip(work, lows):
            mixed = dot(weights, value_ref[rows, lanes])
            mixed_ref[rows, lanes] = jnp.where(low, mixed[:block], mixed[block:]).astype(BF16)
    weight_ref.flush()
    mixed_ref.flush()
    resid = inputs + dot(mixed_ref[...], out_w_ref[...])
    resid_ref[...] = resid
    resid_ref.flush()
    hat, _ = norm_rows(resid)
    second = (hat * gain_two_ref[...] + shift_two_ref[...]).astype(BF16)
    sent_ref[...] = dot(spread_ref[...], second).astype(BF16)


def dispatch_kernel(spread_ref, second_ref, sent_ref):
    sent_ref[...] = dot(spread_ref[...], second_ref[...]).astype(BF16)


def forward_kernel(experts, tile, me_ref, rows_ref, router_ref, up_bias_ref, *refs):
    ups = refs[:-5]
    hidden_ref, slope_ref, gate_ref, gates_ref, inner_s = refs[-5:]
    total = rows_ref.shape[0]
    chunk = 16
    root = math.sqrt(2.0 / math.pi)

    def project(step):
        inner_s[step % 2] = dot(rows_ref[...], ups[step][...])

    lane = lax.broadcasted_iota(jnp.int32, (total, LANES), 1)
    logits = dot_nt(rows_ref[...], router_ref[...])
    project(0)
    logits = jnp.where(lane < experts, logits, -1e30)
    powers = jnp.exp(logits - jnp.max(logits, axis=-1, keepdims=True))
    gates = powers / jnp.sum(powers, axis=-1, keepdims=True)
    gates_ref[...] = gates
    gates_ref.flush()
    gate = jnp.sum(jnp.where(lane == me_ref[0], gates, 0.0), axis=-1, keepdims=True)
    gate_ref[...] = jnp.broadcast_to(gate, (total, LANES))
    gate_ref.flush()
    for step in range(len(ups)):
        if step + 1 < len(ups):
            project(step + 1)
        lanes = slice(step * tile, (step + 1) * tile)
        bias = up_bias_ref[:, lanes]
        for start in range(0, total, chunk):
            at = slice(start, start + chunk)
            inner = inner_s[step % 2, at, :] + bias
            square = inner * inner
            half = 0.5 + 0.5 * jnp.tanh(inner * (root + (root * 0.044715) * square))
            hidden = inner * half
            slope = half + (hidden - hidden * half) * (2.0 * root + (6.0 * root * 0.044715) * square)
            hidden_ref[at, lanes] = hidden.astype(BF16)
            slope_ref[at, lanes] = slope.astype(BF16)
        hidden_ref.flush(slice(None), lanes)
        slope_ref.flush(slice(None), lanes)


def produce_kernel(hidden_ref, down_ref, down_bias_ref, gate_ref, out_ref, *refs):
    parts, total_s = refs[:-1], refs[-1]
    step = pl.program_id(0)
    made = dot(hidden_ref[...], down_ref[...])

    @pl.when(step == 0)
    def _():
        total_s[...] = made

    @pl.when(step > 0)
    def _():
        total_s[...] += made

    @pl.when(step == pl.num_programs(0) - 1)
    def _():
        produced = (total_s[...] + down_bias_ref[...]).astype(BF16)
        out_ref[...] = produced
        size = parts[0].shape[1]
        gate = jnp.concatenate([gate_ref[...]] * (size // LANES), axis=1)
        for at, ref in enumerate(parts):
            ref[...] = (produced[:, at * size : (at + 1) * size].astype(F32) * gate).astype(BF16)


def expert_kernel(experts, tile, me_ref, grad_ref, gate_ref, *refs):
    steps = (len(refs) - 6) // 3
    downs, slopes, ups = [refs[0], *refs[6 : 3 * steps + 3 : 3]], [refs[1], *refs[7 : 3 * steps + 3 : 3]], [refs[2], *refs[8 : 3 * steps + 3 : 3]]
    produced_ref, gates_ref, router_ref = refs[3:6]
    inner_grad_ref, rows_grad_ref, logit_grad_ref = refs[3 * steps + 3 :]
    total, width = grad_ref.shape
    gate = jnp.concatenate([gate_ref[...]] * (tile // LANES), axis=1)
    for step in range(steps):
        lanes = slice(step * tile, (step + 1) * tile)
        made = dot_nt(grad_ref[...], downs[step][...]) * gate * slopes[step][...].astype(F32)
        inner_grad_ref[:, lanes] = made.astype(BF16)
        inner_grad_ref.flush(slice(None), lanes)
        if step == 0:
            lane = lax.broadcasted_iota(jnp.int32, (total, LANES), 1)
            product = grad_ref[...].astype(F32) * produced_ref[...].astype(F32)
            pair_grad = jnp.sum(product, axis=-1, keepdims=True)
            own = jnp.where(lane == me_ref[0], 1.0, 0.0)
            logit_grad = (gates_ref[...] * (own - gate_ref[...]) * pair_grad).astype(BF16)
            logit_grad_ref[...] = logit_grad
            logit_grad_ref.flush()
    made = dot(logit_grad, router_ref[...])
    for step in range(steps):
        made = made + dot_nt(inner_grad_ref[:, step * tile : (step + 1) * tile], ups[step][...])
    rows_grad_ref[...] = made.astype(BF16)


def weight_kernel(sets, again, *refs):
    groups, refs = [refs[at * 5 : at * 5 + 5] for at in range(sets)], refs[5 * sets :]
    earlier, refs = refs[:again], refs[again:]
    extra_ref, out_ref, refs = refs[0], refs[1], refs[2:]
    router_refs, gated_s, inner_grad_s, back_s = refs[:-3], refs[-3], refs[-2], refs[-1]
    total, width = groups[0][0].shape
    chunk = 16

    @pl.when(pl.program_id(0) == 0)
    def _():
        for at, some in enumerate(groups):
            gate = jnp.concatenate([some[2][...]] * (width // LANES), axis=1)
            gated_s[at] = (gate * some[1][...].astype(F32)).astype(BF16)
        if router_refs:
            router_refs[0][...] = dot_tn(extra_ref[...], groups[0][0][...])[: router_refs[0].shape[0]]

    ones = jnp.ones((16, total), BF16)
    ups, downs, up_biases, down_biases = [], [], [], []
    for at, (rows_ref, grad_ref, gate_ref, hidden_ref, inner_grad_ref) in enumerate(groups):
        if again:
            slope_ref, inner_grad_ref = inner_grad_ref, inner_grad_s
            back_s[...] = dot_nt(grad_ref[...], extra_ref[...])
            for start in range(0, total, chunk):
                here = slice(start, start + chunk)
                gate = jnp.concatenate([gate_ref[here, :]] * (width // LANES), axis=1)
                made = back_s[here, :] * gate * slope_ref[here, :].astype(F32)
                inner_grad_s[here, :] = made.astype(BF16)
        inner_grad = inner_grad_ref[...]
        ups.append(dot_tn(rows_ref[...], inner_grad))
        downs.append(dot_tn(hidden_ref[...], gated_s[at]))
        up_biases.append(dot(ones, inner_grad))
        down_biases.append(dot(ones, gated_s[at]))

    def put(some, parts):
        made = sum(parts[1:], parts[0]).astype(BF16)
        if again:
            made = (made.astype(F32) + earlier[0][0, some, :].astype(F32)).astype(BF16)
        out_ref[0, some, :] = made

    put(slice(0, width), ups)
    put(slice(width, 2 * width), downs)
    row = lax.broadcasted_iota(jnp.int32, (16, width), 0)
    small = jnp.where(row == 0, sum(up_biases[1:], up_biases[0]), sum(down_biases[1:], down_biases[0]))
    put(slice(2 * width, None), [small])


def finish_experts_kernel(*refs):
    parts, (up_ref, up_bias_ref, down_ref, down_bias_ref) = refs[:2], refs[-4:]
    tall = up_ref.shape[0]

    def total(some):
        return sum_in_tree([ref[0, some, :].astype(F32) for ref in parts])

    up_ref[...] = total(slice(0, tall))
    down_ref[...] = total(slice(tall, 2 * tall))
    small = total(slice(2 * tall, None))
    up_bias_ref[...] = small[0:1]
    down_bias_ref[...] = small[1:2]


def one_hot_rows(target_ref, slots_all):
    count = target_ref.shape[0]
    lane = lax.broadcasted_iota(jnp.int32, (64, slots_all), 1).astype(F32)
    pieces = []
    for start in range(0, count, 64):
        one = target_ref[start : start + 64, 0:1]
        two = target_ref[start : start + 64, 1:2]
        pieces.append(jnp.where((lane == one) | (lane == two), 1.0, 0.0).astype(BF16))
    return jnp.concatenate(pieces, axis=0)


def combine_kernel(target_ref, resid_ref, *refs):
    parts, out_ref = refs[:-1], refs[-1]
    picked = one_hot_rows(target_ref, parts[0].shape[0])
    size = parts[0].shape[1]
    for at, ref in enumerate(parts):
        lanes = slice(at * size, (at + 1) * size)
        out_ref[:, lanes] = (resid_ref[:, lanes] + dot(picked, ref[...])).astype(BF16)


def backward_kernel(
    experts,
    core_ref,
    back_ref,
    target_ref,
    resid_ref,
    gain_two_ref,
    grad_ref,
    mixed_ref,
    out_w_ref,
    value_ref,
    query_ref,
    weight_ref,
    key_ref,
    normed_ref,
    query_w_ref,
    key_w_ref,
    value_w_ref,
    tokens_ref,
    gain_one_ref,
    count_ref,
    router_grad_ref,
    keep_ref,
    send_ref,
    tokens_grad_ref,
    queries_s,
    keys_s,
    values_s,
    mixed_grad_s,
    resid_grad_s,
):
    count, width = grad_ref.shape
    picked = one_hot_rows(target_ref, back_ref.shape[0])
    second_grad = dot(picked, back_ref[...])
    hat, rate = norm_rows(resid_ref[...])
    gain_two_grad = jnp.sum(second_grad * hat, axis=0, keepdims=True)
    shift_two_grad = jnp.sum(second_grad, axis=0, keepdims=True)
    resid_grad_s[...] = grad_ref[...].astype(F32) + norm_back(hat, rate, gain_two_ref[...], second_grad)
    branch = resid_grad_s[...].astype(BF16)
    half = width // 2
    first = core_ref[0] == 0

    def put(at, value):
        value = value.astype(BF16)
        keep_ref[at * half : (at + 1) * half, :] = jnp.where(first, value[:half], value[half:])
        send_ref[at * half : (at + 1) * half, :] = jnp.where(first, value[half:], value[:half])
        keep_ref.flush(slice(at * half, (at + 1) * half))

    put(3, dot_tn(mixed_ref[...], branch))
    mixed_grad_s[...] = dot_nt(branch, out_w_ref[...]).astype(BF16)
    pairs = HEADS // 2
    wide = width // pairs
    block = 2 * PATCHES
    scale = 1.0 / math.sqrt(width // HEADS)
    low = head_masks(wide)
    together = 8
    cells = [(item, pair) for item in range(count // block) for pair in range(pairs)]
    for start in range(0, len(cells), together):
        work = []
        for item, pair in cells[start : start + together]:
            rows = slice(item * block, (item + 1) * block)
            lanes = slice(pair * wide, (pair + 1) * wide)
            mixed_stack = stack_heads(mixed_grad_s[rows, lanes], low)
            weights = weight_ref[item, pair]
            work.append((rows, lanes, mixed_stack, weights, dot_nt(mixed_stack, value_ref[rows, lanes])))
        score_grads = []
        for rows, lanes, mixed_stack, weights, weight_grad in work:
            product = weights.astype(F32) * weight_grad
            score_grad = product - weights.astype(F32) * jnp.sum(product, axis=-1, keepdims=True)
            score_grads.append(score_grad.astype(BF16))
        for rows, lanes, mixed_stack, weights, _ in work:
            values_s[rows, lanes] = dot_tn(weights, mixed_stack).astype(BF16)
        for (rows, lanes, *_), score_grad in zip(work, score_grads):
            made = dot(score_grad, key_ref[rows, lanes]) * scale
            queries_s[rows, lanes] = jnp.where(low, made[:block], made[block:]).astype(BF16)
        for (rows, lanes, *_), score_grad in zip(work, score_grads):
            keys_s[rows, lanes] = dot_tn(score_grad, stack_heads(query_ref[rows, lanes], low)).astype(BF16)
    normed = normed_ref[...]
    put(0, dot_tn(normed, queries_s[...]))
    put(1, dot_tn(normed, keys_s[...]))
    put(2, dot_tn(normed, values_s[...]))
    normed_grad = (
        dot_nt(queries_s[...], query_w_ref[...])
        + dot_nt(keys_s[...], key_w_ref[...])
        + dot_nt(values_s[...], value_w_ref[...])
    )
    hat, rate = norm_rows(tokens_ref[...].astype(F32))
    gain_one_grad = jnp.sum(normed_grad * hat, axis=0, keepdims=True)
    shift_one_grad = jnp.sum(normed_grad, axis=0, keepdims=True)
    tokens_grad_ref[...] = (resid_grad_s[...] + norm_back(hat, rate, gain_one_ref[...], normed_grad)).astype(BF16)
    tokens_grad_ref.flush()
    digits = []
    for kind in range(2):
        value = count_ref[kind : kind + 1, :]
        high = jnp.floor(value * (1.0 / 128.0))
        digits.append(jnp.concatenate([value - 128.0 * high, high] + [jnp.zeros_like(value)] * (width // LANES - 2), axis=1))
    extra = keep_ref.shape[0] - 4 * half
    small = [gain_one_grad, shift_one_grad, gain_two_grad, shift_two_grad] + digits + [router_grad_ref[:experts, :]]
    small = jnp.concatenate(small + [jnp.zeros((extra - 6 - experts, width), F32)], axis=0).astype(BF16)
    keep_ref[4 * half :, :] = small
    send_ref[4 * half :, :] = small
    keep_ref.flush(slice(4 * half, None))


def carry_digits(total):
    row = lax.broadcasted_iota(jnp.int32, (total.shape[0], LANES), 0)
    one, two, three = (total[:, at * LANES : (at + 1) * LANES] for at in range(3))
    over = jnp.floor(one * (1.0 / 128.0))
    two_full = two + over
    over_two = jnp.floor(two_full * (1.0 / 128.0))
    parts = [one - 128.0 * over, two_full - 128.0 * over_two, three + over_two]
    is_count = (row == 4) | (row == 5)
    parts = [jnp.where(is_count, part, total[:, at * LANES : (at + 1) * LANES]) for at, part in enumerate(parts)]
    return jnp.concatenate(parts + [total[:, 3 * LANES :]], axis=1)


def sum_in_tree(values):
    while len(values) > 1:
        values = [values[at] + values[at + 1] for at in range(0, len(values), 2)]
    return values[0]


def share_kernel(given, pieces, *refs):
    index_ref, arrived, made = refs[0], refs[1 : 1 + given], refs[1 + given :]
    small_rows = (pieces * made[0].shape[0] - arrived[0].shape[0]) // (pieces - 1)
    size = made[0].shape[0] - small_rows
    top = pieces * size
    small = carry_digits(sum_in_tree([ref[top:, :].astype(F32) for ref in arrived])).astype(BF16)
    for away in range(pieces):
        at = pl.ds(pl.multiple_of((index_ref[0] ^ away) * size, size), size)
        made[away][:size, :] = sum_in_tree([ref[at, :].astype(F32) for ref in arrived]).astype(BF16)
        made[away][size:, :] = small


def copy_kernel(given_ref, made_ref, arrival):
    copy = pltpu.make_async_copy(given_ref, made_ref, arrival)
    copy.start()
    copy.wait()


def pass_kernel(given_ref, same_ref):
    pass


def gather_kernel(*refs):
    arrived, out_ref = refs[:-1], refs[-1]
    size = arrived[0].shape[0]
    for at, ref in enumerate(arrived):
        out_ref[at * size : (at + 1) * size, :] = ref[...]


def last_kernel(given, *refs):
    arrived, chunk_ref, small_ref = refs[:given], refs[given], refs[given + 1]
    size = chunk_ref.shape[0]
    chunk_ref[...] = sum_in_tree([ref[:size, :].astype(F32) for ref in arrived]).astype(BF16)
    small_ref[...] = carry_digits(sum_in_tree([ref[size:, :].astype(F32) for ref in arrived])).astype(BF16)


def finish_shared_kernel(experts, index_ref, *refs):
    own, others, small_ref, outs = refs[:4], refs[4:8], refs[8], refs[9:]
    vector_refs, router_ref, count_ref = outs[4:8], outs[8], outs[9]
    core, place, inner_place = index_ref[0], index_ref[1], index_ref[2]
    half = outs[0].shape[1] // 2
    size = half // 4
    for pieces, side in ((own, core), (others, 1 - core)):
        for away, piece in enumerate(pieces):
            for at in range(4):

                @pl.when((place ^ away) == at)
                def _(piece=piece, side=side, out=outs[at]):
                    for part in range(4):
                        start = pl.multiple_of((inner_place ^ part) * size, size)
                        row = pl.multiple_of(side * half + part * size, size)
                        out[pl.ds(row, size), :] = piece[pl.ds(start, size), :].astype(F32)

    small = small_ref[...].astype(F32)
    for at, ref in enumerate(vector_refs):
        ref[...] = small[at : at + 1, :]
    router_ref[...] = small[6 : 6 + experts, :]
    value = small[4:6, :LANES] + 128.0 * small[4:6, LANES : 2 * LANES] + 16384.0 * small[4:6, 2 * LANES : 3 * LANES]
    count_ref[...] = value[:, :experts].astype(jnp.int32)


def solution(mesh):
    narrow, wide = mesh.shape["narrow"], mesh.shape["wide"]

    def hop(value, narrow_bits, wide_bits):
        if wide_bits == 0:
            return lax.ppermute(value, "narrow", [(i, i ^ narrow_bits) for i in range(narrow)])
        if narrow_bits == 0:
            return lax.ppermute(value, "wide", [(i, i ^ wide_bits) for i in range(wide)])
        pairs = [
            (i * wide + j, (i ^ narrow_bits) * wide + (j ^ wide_bits)) for i in range(narrow) for j in range(wide)
        ]
        return lax.ppermute(value, ("narrow", "wide"), pairs)

    def body(
        tokens,
        gain_one,
        shift_one,
        query_w,
        key_w,
        value_w,
        out_w,
        gain_two,
        shift_two,
        router_w,
        up_w,
        up_bias,
        down_w,
        down_bias,
        picks,
        ranks,
        out_grad,
    ):
        count, width = tokens.shape
        experts = router_w.shape[1]
        capacity = ((21 * 2 * count + 20 * experts - 1) // (20 * experts) + 7) // 8 * 8
        slots_all = experts * capacity
        hidden_width = up_w.shape[2]
        half = width // 2
        pairs = HEADS // 2
        blocks = count // (2 * PATCHES)
        extra = (6 + experts + 15) // 16 * 16
        tile = width
        steps = hidden_width // tile
        narrow_at, wide_at = lax.axis_index("narrow"), lax.axis_index("wide")
        core = (narrow_at & 1)[None].astype(jnp.int32)
        place = (((narrow_at >> 1) & 1) * 2 + (wide_at & 1))[None].astype(jnp.int32)
        inner_place = ((wide_at >> 1) & 3)[None].astype(jnp.int32)
        gain_one, shift_one, gain_two, shift_two = (v[None, :] for v in (gain_one, shift_one, gain_two, shift_two))
        router_t = jnp.pad(router_w.T, ((0, LANES - experts), (0, 0)))
        up_w, down_w = up_w[0], down_w[0]

        def exchange(value):
            return lax.all_to_all(value, "wide", split_axis=0, concat_axis=0, tiled=True)

        token_rows = shape((count, width), BF16)
        rows_shape = shape((slots_all, width), BF16)
        lanes_shape = shape((slots_all, LANES), F32)
        narrow_far = far((count, width), BF16)
        spread, target, counts, resid, normed, queries, keys, values, weights, mixed, sent = fuse(
            functools.partial(attention_kernel, capacity, experts),
            (tokens, gain_one, shift_one, picks.T, ranks.T, query_w, key_w, value_w, out_w, gain_two, shift_two),
            (
                far((slots_all, count), BF16),
                far((count, 8), F32),
                far((8, LANES), F32),
                far((count, width), F32),
                narrow_far,
                narrow_far,
                narrow_far,
                narrow_far,
                far((blocks, pairs, 4 * PATCHES, 2 * PATCHES), BF16),
                narrow_far,
                held((slots_all, width), BF16),
            ),
            32,
            10,
            "attention",
        )
        rows = exchange(sent)
        (grad_sent,) = run(dispatch_kernel, (spread, out_grad), (rows_shape,), 16, 1, "dispatch", after=(Held(sent),))
        grad_rows = exchange(grad_sent)

        whole = pl.BlockSpec((slots_all, width), lambda f: (0, 0))
        lanes_whole = pl.BlockSpec((slots_all, LANES), lambda f: (0, 0))
        columns = pl.BlockSpec((slots_all, tile), lambda f: (0, f))
        down_spec = pl.BlockSpec((tile, width), lambda f: (f, 0))
        down_bias_spec = pl.BlockSpec((1, width), lambda f: (0, 0))
        payload = 2 * width + 16
        me = wide_at[None].astype(jnp.int32)
        rows = Held(rows)

        def forward(rows, us, after=()):
            return fuse(
                functools.partial(forward_kernel, experts, tile),
                (me, rows, router_t, up_bias) + tuple(Part(up_w, tile, at) for at in range(steps)),
                (far((slots_all, hidden_width), BF16),) * 2 + (far((slots_all, LANES), F32),) * 2,
                32,
                us,
                "forward",
                (pltpu.VMEM((2, slots_all, tile), F32),),
                after=after,
            )

        hidden, slope, gate, gates = forward(rows, 0.01)
        produced, gated = run(
            produce_kernel,
            (hidden, down_w, down_bias, gate),
            (rows_shape,) * 2,
            32,
            0.01,
            "produce",
            (pltpu.VMEM((slots_all, width), F32),),
            grid=(steps,),
            in_specs=(columns, down_spec, down_bias_spec, lanes_whole),
            out_specs=(whole,) * 2,
        )
        grad_rows = Held(grad_rows)

        def triple(at):
            return Part(down_w, tile, at, rows=True), Part(slope, tile, at), Part(up_w, tile, at)

        rows_others = [hop(rows.value, bits, 0) for bits in range(2, narrow, 2)]
        inner_grad, rows_grad, logit_grad = fuse(
            functools.partial(expert_kernel, experts, tile),
            (me, grad_rows, gate, *triple(0), produced, gates, router_t, *(part for at in range(1, steps) for part in triple(at))),
            (far((slots_all, hidden_width), BF16), held((slots_all, width), BF16), far((slots_all, LANES), BF16)),
            40,
            0.01,
            "experts",
            after=[Held(one) for one in rows_others],
        )
        back = exchange(rows_grad)

        def payload_of(number):
            return shape((number, payload, width), BF16)

        payload_spec = pl.BlockSpec((1, payload, width), lambda f: (f, 0, 0))
        router_spec = pl.BlockSpec((experts, width), lambda f: (0, 0))
        (grad_later,) = run(
            copy_kernel,
            (grad_rows,),
            (rows_shape,),
            4,
            0.01,
            "copy_rows",
            (pltpu.SemaphoreType.DMA,),
            in_specs=(pl.BlockSpec(memory_space=pl.ANY),),
            out_specs=(pl.BlockSpec(memory_space=pltpu.HBM),),
            after=(produced,),
        )

        def held_back(value, after, space=pltpu.HBM):
            return run(
                pass_kernel,
                (value if space == pltpu.HBM else Held(value),),
                (value,),
                1,
                0.01,
                "pass",
                in_specs=(pl.BlockSpec(memory_space=space),),
                out_specs=(pl.BlockSpec(memory_space=space),),
                after=after,
                free=space != pltpu.HBM,
                input_output_aliases={0: 0},
            )[0]

        sets = []
        for bits, rows_of in zip(range(2, narrow, 2), rows_others):
            grad_of = hop(grad_later, bits, 0)
            hidden_of, slope_of, gate_of, _ = forward(rows_of, 0.01, (logit_grad,))
            sets.append((rows_of, grad_of, gate_of, hidden_of, slope_of))

        def weight_part(again, sets, extra, extra_spec, earlier=(), after=()):
            return run(
                functools.partial(weight_kernel, len(sets), int(again)),
                (*(item for one in sets for item in one), *earlier, extra),
                (payload_of(steps),) + (shape((experts, width), F32),) * (not again),
                48,
                0.01,
                "expert_weights",
                (
                    pltpu.VMEM((len(sets), slots_all, width), BF16),
                    pltpu.VMEM((slots_all, tile), BF16),
                    pltpu.VMEM((slots_all, tile), F32),
                ),
                grid=(steps,),
                in_specs=(
                    *(spec for _ in sets for spec in (whole, whole, lanes_whole, columns, columns)),
                    *(payload_spec for _ in earlier),
                    extra_spec,
                ),
                out_specs=(payload_spec,) + (router_spec,) * (not again),
                after=after,
            )

        def finish_experts(start, number, parts, earlier, after=()):
            spec = lambda dims, index: pl.BlockSpec(dims, lambda f: index(start + f))
            return run(
                finish_experts_kernel,
                (*parts, *earlier),
                (
                    shape((width, hidden_width), F32),
                    shape((1, hidden_width), F32),
                    shape((hidden_width, width), F32),
                    shape((1, width), F32),
                ),
                32,
                0.01,
                "finish_experts",
                grid=(number,),
                in_specs=[pl.BlockSpec((1, payload, width), lambda f: (start + f, 0, 0))] * 2
                + [pl.BlockSpec(memory_space=pltpu.HBM)] * len(earlier),
                out_specs=(
                    spec((width, tile), lambda f: (0, f)),
                    spec((1, tile), lambda f: (0, f)),
                    spec((tile, width), lambda f: (f, 0)),
                    down_bias_spec,
                ),
                after=after,
                input_output_aliases={2 + at: at for at in range(len(earlier))},
            )

        own_sum, router_part = weight_part(
            False, [(rows, grad_rows, gate, hidden, inner_grad)], logit_grad, lanes_whole, (), [one[4] for one in sets]
        )
        produced_back = exchange(held_back(gated, (own_sum,)))
        tall = 4 * half + extra
        keep, send, tokens_grad = fuse(
            functools.partial(backward_kernel, experts),
            (
                core,
                Held(back),
                target,
                resid,
                gain_two,
                out_grad,
                mixed,
                out_w,
                values,
                queries,
                weights,
                keys,
                normed,
                query_w,
                key_w,
                value_w,
                tokens,
                gain_one,
                counts,
                router_part,
            ),
            (far((tall, width), BF16), held((tall, width), BF16), far((count, width), BF16)),
            32,
            0.01,
            "backward",
            [pltpu.VMEM((count, width), BF16)] * 4 + [pltpu.VMEM((count, width), F32)],
            after=[own_sum] + [Held(one[1]) for one in sets],
        )

        def share(index, arrived, after=()):
            size = (arrived[0].shape[0] - extra) // 4
            return run(
                functools.partial(share_kernel, len(arrived), 4),
                (index, arrived[0] if size == half else Held(arrived[0]), *map(Held, arrived[1:])),
                (shape((size + extra, width), BF16),) * 4,
                16,
                0.05,
                "share",
                after=after,
                free=True,
            )

        def last(arrived, after=()):
            return run(
                functools.partial(last_kernel, len(arrived)),
                tuple(map(Held, arrived)),
                (shape((half // 4, width), BF16), shape((extra, width), BF16)),
                16,
                0.05,
                "last",
                after=after,
                free=True,
            )

        def gather(arrived, after=()):
            rows_in = sum(value.shape[0] for value in arrived)
            return run(
                gather_kernel,
                tuple(map(Held, arrived)),
                (shape((rows_in, width), BF16),),
                16,
                0.05,
                "gather",
                after=after,
                free=True,
            )[0]

        def spread_out(parts, bits):
            return [parts[0]] + [hop(part, *bit) for part, bit in zip(parts[1:], bits[1:])]

        places = ((0, 0), (0, 1), (2, 0), (2, 1))
        inner_places = ((0, 0), (0, 2), (0, 4), (0, 6))
        parts = share(place, [keep, hop(send, 1, 0)])
        (far_sum,) = weight_part(True, sets, down_w, down_spec, (own_sum,), (Held(parts[0]),))
        parts = share(inner_place, spread_out(parts, places), (far_sum, Held(produced_back)))
        far_sum = held_back(far_sum, (Held(parts[0]),))
        parts = spread_out(parts, inner_places)
        (block_out,) = run(
            combine_kernel, (target, resid, Held(produced_back)), (token_rows,), 16, 0.01, "combine"
        )
        chunk, small = last(parts, (block_out,))
        others = [(bit, 0) for bit in (4, 8, 16, 32, 64) if bit < narrow]
        others += [(0, bit) for bit in (8, 16, 32, 64) if bit < wide]
        for bits in others:
            joined = jnp.concatenate([chunk, small], axis=0)
            chunk, small = last([joined, hop(joined, *bits)])
        sums = (far_sum, Held(hop(far_sum, 1, 0)))
        finished = finish_experts(0, steps // 2, sums, (), (Held(chunk),))
        chunk = gather(spread_out([chunk] * 4, inner_places), (finished[0],))
        pieces = spread_out([chunk] * 4, places)
        finished = finish_experts(steps // 2, steps - steps // 2, sums, finished, (Held(chunk),))
        pieces[3] = held_back(pieces[3], finished[:1], pl.ANY)
        up_grad, up_bias_grad, down_grad, down_bias_grad = finished
        outs = run(
            functools.partial(finish_shared_kernel, experts),
            (
                jnp.concatenate([core, place, inner_place]),
                *map(Held, pieces),
                *(Held(hop(piece, 1, 0)) for piece in pieces),
                Held(small),
            ),
            (shape((width, width), F32),) * 4
            + (shape((1, width), F32),) * 4
            + (shape((experts, width), F32), shape((2, experts), jnp.int32)),
            32,
            3,
            "finish_shared",
        )
        query_grad, key_grad, value_grad, out_w_grad, g_one, s_one, g_two, s_two, router_grad, tallies = outs
        return (
            block_out,
            tokens_grad,
            g_one[0],
            s_one[0],
            query_grad,
            key_grad,
            value_grad,
            out_w_grad,
            g_two[0],
            s_two[0],
            router_grad.T,
            up_grad[None],
            up_bias_grad,
            down_grad[None],
            down_bias_grad,
            tallies.T,
        )

    tokens_spec = P(("narrow", "wide"), None)
    in_specs = (
        (tokens_spec,)
        + (P(),) * 9
        + (P("wide", None, None), P("wide", None), P("wide", None, None), P("wide", None))
        + (tokens_spec,) * 3
    )
    out_specs = (
        (tokens_spec,) * 2
        + (P(),) * 9
        + (P("wide", None, None), P("wide", None), P("wide", None, None), P("wide", None))
        + (P(),)
    )
    return jax.shard_map(body, mesh=mesh, in_specs=in_specs, out_specs=out_specs, check_vma=False)
```

profile of v0, /device:TPU:0, one launch (start us, length us, event | category | flops | bytes accessed | tf_op | source)
XLA Modules:
  0.0 172.7 jit_solution(8125843508195179126)
XLA Ops:
  0.6 8.0 %attention.1 = (bf16[832,384]{1,0:T(8,128)(2,1)}, f32[384,8]{1,0:T(8,128)}, f32[8,128]{1,0:T(8,128)}, f32[384,512]{1,0:T(8,128)}, bf16[384,512]{1,0:T(8,128)(2,1...) custom-call(bf16[384,512]{1,0:T(8,128)(2,1)} %refs_16_.1, ...), custom_call_target="tpu_custom_call" | custom-call | flops 10000000000 | bytes 1000000 | tf_op jit(solution)/shard_map/attention/pallas_call | solution.py:176
  8.7 7.3 %all-to-all-start = ((bf16[8,104,512]{2,1,0:T(8,128)(2,1)}), bf16[8,104,512]{2,1,0:T(8,128)(2,1)S(1)}, u32[]{:S(2)}, u32[]{:S(2)}) async-start(bf16[8,104,512]{2,1,0:T(8,128)(2,1)} %bitcast.7), calls=%async_computation | async-start | bytes 1703936 | tf_op jit(solution)/shard_map/all_to_all | solution.py:738
  16.0 2.7 %dispatch.1 = bf16[832,512]{1,0:T(8,128)(2,1)} custom-call(bf16[832,384]{1,0:T(8,128)(2,1)} %get-tuple-element.78.refs_0_, bf16[384,512]{1,0:T(8,128)(2,1)} %refs_5_.3, bf16[832,512]{1,0:T(8,128)(2,1)} %get-tuple-element.74.refs_2_), custom_call_target="tpu_custom_call" | custom-call | flops 1000000000 | bytes 100000 | tf_op jit(solution)/shard_map/dispatch/pallas_call | solution.py:87
  18.7 18.9 %all-to-all-done = bf16[8,104,512]{2,1,0:T(8,128)(2,1)S(1)} async-done(((bf16[8,104,512]{2,1,0:T(8,128)(2,1)}), bf16[8,104,512]{2,1,0:T(8,128)(2,1)S(1)}, u32[]{:S(2)}, u32[]{:S(2)}) %all-to-all-start) | async-done | bytes 852000 | tf_op jit(solution)/shard_map/all_to_all | solution.py:738
  37.6 3.7 %all-to-all-start.1 = ((bf16[8,104,512]{2,1,0:T(8,128)(2,1)}), bf16[8,104,512]{2,1,0:T(8,128)(2,1)S(1)}, u32[]{:S(2)}, u32[]{:S(2)}) async-start(bf16[8,104,512]{2,1,0:T(8,128)(2,1)} %bitcast.59), calls=%async_computation.1 | async-start | bytes 1703936 | tf_op jit(solution)/shard_map/all_to_all | solution.py:738
  43.6 8.7 %forward.2 = (bf16[832,2048]{1,0:T(8,128)(2,1)}, bf16[832,2048]{1,0:T(8,128)(2,1)}, f32[832,128]{1,0:T(8,128)}, f32[832,128]{1,0:T(8,128)}) custom-call(s32[1]{0:T(128)} %bitcast.6.refs_0_, bf16[832,512]{1,0:T(8,128)(2,1)S(1)} %bitcast.35, bf16[128,512]{1,0:T(8,128)(2,1)} %pad.4.refs_2_.refs_8_, f32[1,2048]{1,0:T(1,128)} %refs_3_.3, ...), custom_call_target="tpu_custom_call" | custom-call | flops 10000000 | bytes 1000 | tf_op jit(solution)/shard_map/forward/pallas_call | solution.py:176
  52.3 6.6 %produce.1 = (bf16[832,512]{1,0:T(8,128)(2,1)}, bf16[832,512]{1,0:T(8,128)(2,1)}) custom-call(bf16[832,2048]{1,0:T(8,128)(2,1)} %get-tuple-element.75.refs_0_.refs_3_, bf16[2048,512]{1,0:T(8,128)(2,1)} %bitcast.50, f32[1,512]{1,0:T(1,128)} %refs_2_.1, f32[832,128]{1,0:T(8,128)} %get-tuple-element.76.refs_3_.refs_2_), custom_call_target="tpu_custom_call" | custom-call | flops 10000000 | bytes 1000 | tf_op jit(solution)/shard_map/produce/pallas_call | solution.py:87
  58.9 4.1 %all-to-all-done.1 = bf16[8,104,512]{2,1,0:T(8,128)(2,1)S(1)} async-done(((bf16[8,104,512]{2,1,0:T(8,128)(2,1)}), bf16[8,104,512]{2,1,0:T(8,128)(2,1)S(1)}, u32[]{:S(2)}, u32[]{:S(2)}) %all-to-all-start.1) | async-done | bytes 852000 | tf_op jit(solution)/shard_map/all_to_all | solution.py:738
  63.0 9.1 %experts.1 = (bf16[832,2048]{1,0:T(8,128)(2,1)}, bf16[832,512]{1,0:T(8,128)(2,1)}, bf16[832,128]{1,0:T(8,128)(2,1)}) custom-call(s32[1]{0:T(128)} %bitcast.6.refs_0_, bf16[832,512]{1,0:T(8,128)(2,1)S(1)} %bitcast.29, f32[832,128]{1,0:T(8,128)} %get-tuple-element.76.refs_3_.refs_2_, bf16[2048,512]{1,0:T(8,128)(2,1)} %bitcast.51, ...), custom_call_target="tpu_custom_call" | custom-call | flops 10000000 | bytes 1000 | tf_op jit(solution)/shard_map/experts/pallas_call | solution.py:176
  72.1 4.5 %all-to-all-start.3 = ((bf16[8,104,512]{2,1,0:T(8,128)(2,1)}), bf16[8,104,512]{2,1,0:T(8,128)(2,1)S(1)}, u32[]{:S(2)}, u32[]{:S(2)}) async-start(bf16[8,104,512]{2,1,0:T(8,128)(2,1)} %bitcast.17), calls=%async_computation.3 | async-start | bytes 1703936 | tf_op jit(solution)/shard_map/all_to_all | solution.py:738
  79.2 9.1 %forward.3 = (bf16[832,2048]{1,0:T(8,128)(2,1)}, bf16[832,2048]{1,0:T(8,128)(2,1)}, f32[832,128]{1,0:T(8,128)}, f32[832,128]{1,0:T(8,128)}) custom-call(s32[1]{0:T(128)} %bitcast.6.refs_0_, bf16[832,512]{1,0:T(8,128)(2,1)} %copy-done, bf16[128,512]{1,0:T(8,128)(2,1)} %pad.4.refs_2_.refs_8_, f32[1,2048]{1,0:T(1,128)} %refs_3_.3, bf16[512,2048]{1,0:T(8,128)(2,1)} %bitcast.46, ...), custom_call_target="tpu_custom_call" | custom-call | flops 10000000 | bytes 1000 | tf_op jit(solution)/shard_map/forward/pallas_call | solution.py:176
  88.2 9.5 %expert_weights.2 = (bf16[4,1040,512]{2,1,0:T(8,128)(2,1)}, f32[8,512]{1,0:T(8,128)}) custom-call(bf16[832,512]{1,0:T(8,128)(2,1)S(1)} %bitcast.36, bf16[832,512]{1,0:T(8,128)(2,1)S(1)} %bitcast.31, f32[832,128]{1,0:T(8,128)} %get-tuple-element.76.refs_3_.refs_2_, bf16[832,2048]{1,0:T(8,128)(2,1)} %get-tuple-element.75.refs_0_.refs_3_, ...), custom_call_target="tpu_custom_call" | custom-call | flops 10000000 | bytes 1000 | tf_op jit(solution)/shard_map/expert_weights/pallas_call | solution.py:87
  97.7 6.0 %all-to-all-start.2 = ((bf16[8,104,512]{2,1,0:T(8,128)(2,1)}), bf16[8,104,512]{2,1,0:T(8,128)(2,1)S(1)}, u32[]{:S(2)}, u32[]{:S(2)}) async-start(bf16[8,104,512]{2,1,0:T(8,128)(2,1)} %bitcast.58), calls=%async_computation.2 | async-start | bytes 1703936 | tf_op jit(solution)/shard_map/all_to_all | solution.py:738
  103.7 9.7 %backward.1 = (bf16[1040,512]{1,0:T(8,128)(2,1)}, bf16[1040,512]{1,0:T(8,128)(2,1)}, bf16[384,512]{1,0:T(8,128)(2,1)}) custom-call(s32[1]{0:T(128)} %bitcast.16.refs_0_, bf16[832,512]{1,0:T(8,128)(2,1)S(1)} %bitcast.37, f32[384,8]{1,0:T(8,128)} %get-tuple-element.72.refs_0_.refs_2_, f32[384,512]{1,0:T(8,128)} %get-tuple-element.73.refs_1_.refs_3_, ...), custom_call_target="tpu_custom_call" | custom-call | flops 10000000 | bytes 1000 | tf_op jit(solution)/shard_map/backward/pallas_call | solution.py:176
  113.6 2.9 %collective-permute-done.2.refs_2_ = bf16[1040,512]{1,0:T(8,128)(2,1)S(1)} collective-permute-done((bf16[1040,512]{1,0:T(8,128)(2,1)}, bf16[1040,512]{1,0:T(8,128)(2,1)S(1)}, u32[]{:S(2)}, u32[]{:S(2)}) %collective-permute-start.2) | collective-permute-done | bytes 1064992 | tf_op jit(solution)/shard_map/ppermute | solution.py:691
  117.9 2.1 %collective-permute-start.3 = (bf16[272,512]{1,0:T(8,128)(2,1)S(1)}, bf16[272,512]{1,0:T(8,128)(2,1)S(1)}, u32[]{:S(2)}, u32[]{:S(2)}) collective-permute-start(bf16[272,512]{1,0:T(8,128)(2,1)S(1)} %get-tuple-element.99), channel_id=1, source_target_pairs={{0,1},{1,0},{2,3},{3,2},{4,5},{5,4},{6,7},{7,6},{8,9},{9,8},{10,11... | collective-permute-start | bytes 835592 | tf_op jit(solution)/shard_map/ppermute | solution.py:693
  121.5 12.1 %expert_weights.3.refs_5_.refs_0_ = bf16[4,1040,512]{2,1,0:T(8,128)(2,1)} custom-call(bf16[832,512]{1,0:T(8,128)(2,1)} %copy-done, bf16[832,512]{1,0:T(8,128)(2,1)} %copy-done.1, f32[832,128]{1,0:T(8,128)} %get-tuple-element.102.refs_2_, bf16[832,2048]{1,0:T(8,128)(2,1)} %get-tuple-element.103.refs_3_, bf16[832,2048]{1,0:T(8,128)(2,1)} %get-tuple-element.84.refs_6_.refs_4_, ...), custom_call_target="tpu_custom_call" | custom-call | flops 10000000 | bytes 1000 | tf_op jit(solution)/shard_map/expert_weights/pallas_call | solution.py:87
  136.1 2.4 %collective-permute-start.7 = (bf16[80,512]{1,0:T(8,128)(2,1)S(1)}, bf16[80,512]{1,0:T(8,128)(2,1)S(1)}, u32[]{:S(2)}, u32[]{:S(2)}) collective-permute-start(bf16[80,512]{1,0:T(8,128)(2,1)S(1)} %get-tuple-element.106), channel_id=1, source_target_pairs={{0,4},{1,5},{2,6},{3,7},{4,0},{5,1},{6,2},{7,3},{8,12},{9,13},{10,... | collective-permute-start | bytes 245768 | tf_op jit(solution)/shard_map/ppermute | solution.py:693
  138.9 2.6 %combine.1.refs_4_ = bf16[384,512]{1,0:T(8,128)(2,1)} custom-call(f32[384,8]{1,0:T(8,128)} %get-tuple-element.72.refs_0_.refs_2_, f32[384,512]{1,0:T(8,128)} %get-tuple-element.73.refs_1_.refs_3_, bf16[832,512]{1,0:T(8,128)(2,1)S(1)} %bitcast.33), custom_call_target="tpu_custom_call" | custom-call | flops 10000000 | bytes 1000 | tf_op jit(solution)/shard_map/combine/pallas_call | solution.py:87
  141.5 4.2 %collective-permute-done.7.refs_2_ = bf16[80,512]{1,0:T(8,128)(2,1)S(1)} collective-permute-done((bf16[80,512]{1,0:T(8,128)(2,1)S(1)}, bf16[80,512]{1,0:T(8,128)(2,1)S(1)}, u32[]{:S(2)}, u32[]{:S(2)}) %collective-permute-start.7) | collective-permute-done | bytes 81952 | tf_op jit(solution)/shard_map/ppermute | solution.py:693
  150.2 3.4 %finish_experts.2 = (f32[512,2048]{1,0:T(8,128)}, f32[1,2048]{1,0:T(1,128)}, f32[2048,512]{1,0:T(8,128)}, f32[1,512]{1,0:T(1,128)}) custom-call(bf16[4,1040,512]{2,1,0:T(8,128)(2,1)} %pass.4.refs_0_, bf16[4,1040,512]{2,1,0:T(8,128)(2,1)S(1)} %collective-permute-done.12.refs_1_, bf16[64,512]{1,0:T(8,128)(2,1)S(1)} %get-tuple-element.108.refs_2_.refs_0_), custom_call_target="tpu_custom_call" | custom-call | flops 10000000 | bytes 1000 | tf_op jit(solution)/shard_map/finish_experts/pallas_call | solution.py:87
  158.7 3.4 %finish_experts.3 = (f32[512,2048]{1,0:T(8,128)}, f32[1,2048]{1,0:T(1,128)}, f32[2048,512]{1,0:T(8,128)}, f32[1,512]{1,0:T(1,128)}) custom-call(bf16[4,1040,512]{2,1,0:T(8,128)(2,1)} %pass.4.refs_0_, bf16[4,1040,512]{2,1,0:T(8,128)(2,1)S(1)} %collective-permute-done.12.refs_1_, ...), custom_call_target="tpu_custom_call", output_to_operand_aliasing={{0}: (2, {}), {1}: (3, {}), {2}: (4, {}), {3}: (5, {})} | custom-call | flops 10000000 | bytes 1000 | tf_op jit(solution)/shard_map/finish_experts/pallas_call | solution.py:87
  165.4 2.8 %collective-permute-done.15.refs_0_ = bf16[256,512]{1,0:T(8,128)(2,1)S(1)} collective-permute-done((bf16[256,512]{1,0:T(8,128)(2,1)S(1)}, bf16[256,512]{1,0:T(8,128)(2,1)S(1)}, u32[]{:S(2)}, u32[]{:S(2)}) %collective-permute-start.15) | collective-permute-done | bytes 262176 | tf_op jit(solution)/shard_map/ppermute | solution.py:697
  169.7 3.0 %finish_shared.1 = (f32[512,512]{1,0:T(8,128)}, f32[512,512]{1,0:T(8,128)}, f32[512,512]{1,0:T(8,128)}, f32[512,512]{1,0:T(8,128)}, f32[1,512]{1,0:T(1,128)}, /*...) custom-call(s32[3]{0:T(128)S(1)} %pad_add_fusion.refs_0_, ...), custom_call_target="tpu_custom_call" | custom-call | flops 3000000000 | bytes 300000 | tf_op jit(solution)/shard_map/finish_shared/pallas_call | solution.py:87
  (53 shorter events, 25.1 us)
Async XLA Ops:
  8.7 28.9 %all-to-all-start = ((bf16[8,104,512]{2,1,0:T(8,128)(2,1)}), bf16[8,104,512]{2,1,0:T(8,128)(2,1)S(1)}, u32[]{:S(2)}, u32[]{:S(2)}) async-start(bf16[8,104,512]{2,1,0:T(8,128)(2,1)} %bitcast.7), calls=%async_computation | async-start | bytes 1703936 | tf_op jit(solution)/shard_map/all_to_all | solution.py:738
  37.6 25.3 %all-to-all-start.1 = ((bf16[8,104,512]{2,1,0:T(8,128)(2,1)}), bf16[8,104,512]{2,1,0:T(8,128)(2,1)S(1)}, u32[]{:S(2)}, u32[]{:S(2)}) async-start(bf16[8,104,512]{2,1,0:T(8,128)(2,1)} %bitcast.59), calls=%async_computation.1 | async-start | bytes 1703936 | tf_op jit(solution)/shard_map/all_to_all | solution.py:738
  41.4 21.6 %collective-permute-start = (bf16[832,512]{1,0:T(8,128)(2,1)S(1)}, bf16[832,512]{1,0:T(8,128)(2,1)S(1)}, u32[]{:S(2)}, u32[]{:S(2)}) collective-permute-start(bf16[832,512]{1,0:T(8,128)(2,1)S(1)} %bitcast.34), channel_id=1, source_target_pairs={{0,16},{8,24},{16,0},{24,8},{1,17},{9,25},{17,1},{25,9},{2,18},{10... | collective-permute-start | bytes 2555912 | tf_op jit(solution)/shard_map/ppermute | solution.py:691
  72.1 25.6 %all-to-all-start.3 = ((bf16[8,104,512]{2,1,0:T(8,128)(2,1)}), bf16[8,104,512]{2,1,0:T(8,128)(2,1)S(1)}, u32[]{:S(2)}, u32[]{:S(2)}) async-start(bf16[8,104,512]{2,1,0:T(8,128)(2,1)} %bitcast.17), calls=%async_computation.3 | async-start | bytes 1703936 | tf_op jit(solution)/shard_map/all_to_all | solution.py:738
  77.6 26.1 %collective-permute-start.1 = (bf16[832,512]{1,0:T(8,128)(2,1)}, bf16[832,512]{1,0:T(8,128)(2,1)S(1)}, u32[]{:S(2)}, u32[]{:S(2)}) collective-permute-start(bf16[832,512]{1,0:T(8,128)(2,1)} %copy_rows.1), channel_id=1, source_target_pairs={{0,16},{8,24},{16,0},{24,8},{1,17},{9,25},{17,1},{25,9},{2,18},{10... | collective-permute-start | bytes 2555912 | tf_op jit(solution)/shard_map/ppermute | solution.py:691
  97.7 35.9 %all-to-all-start.2 = ((bf16[8,104,512]{2,1,0:T(8,128)(2,1)}), bf16[8,104,512]{2,1,0:T(8,128)(2,1)S(1)}, u32[]{:S(2)}, u32[]{:S(2)}) async-start(bf16[8,104,512]{2,1,0:T(8,128)(2,1)} %bitcast.58), calls=%async_computation.2 | async-start | bytes 1703936 | tf_op jit(solution)/shard_map/all_to_all | solution.py:738
  113.5 3.0 %collective-permute-start.2 = (bf16[1040,512]{1,0:T(8,128)(2,1)}, bf16[1040,512]{1,0:T(8,128)(2,1)S(1)}, u32[]{:S(2)}, u32[]{:S(2)}) collective-permute-start(bf16[1040,512]{1,0:T(8,128)(2,1)} %get-tuple-element.97), channel_id=1, source_target_pairs={{0,8},{8,0},{16,24},{24,16},{1,9},{9,1},{17,25},{25,17},{2,10},{10... | collective-permute-start | bytes 3194888 | tf_op jit(solution)/shard_map/ppermute | solution.py:691
  117.9 15.7 %collective-permute-start.3 = (bf16[272,512]{1,0:T(8,128)(2,1)S(1)}, bf16[272,512]{1,0:T(8,128)(2,1)S(1)}, u32[]{:S(2)}, u32[]{:S(2)}) collective-permute-start(bf16[272,512]{1,0:T(8,128)(2,1)S(1)} %get-tuple-element.99), channel_id=1, source_target_pairs={{0,1},{1,0},{2,3},{3,2},{4,5},{5,4},{6,7},{7,6},{8,9},{9,8},{10,11... | collective-permute-start | bytes 835592 | tf_op jit(solution)/shard_map/ppermute | solution.py:693
  120.0 13.6 %collective-permute-start.4 = (bf16[272,512]{1,0:T(8,128)(2,1)S(1)}, bf16[272,512]{1,0:T(8,128)(2,1)S(1)}, u32[]{:S(2)}, u32[]{:S(2)}) collective-permute-start(bf16[272,512]{1,0:T(8,128)(2,1)S(1)} %get-tuple-element.100), channel_id=1, source_target_pairs={{0,16},{8,24},{16,0},{24,8},{1,17},{9,25},{17,1},{25,9},{2,18},{10... | collective-permute-start | bytes 835592 | tf_op jit(solution)/shard_map/ppermute | solution.py:691
  120.5 13.7 %collective-permute-start.5 = (bf16[272,512]{1,0:T(8,128)(2,1)S(1)}, bf16[272,512]{1,0:T(8,128)(2,1)S(1)}, u32[]{:S(2)}, u32[]{:S(2)}) collective-permute-start(bf16[272,512]{1,0:T(8,128)(2,1)S(1)} %get-tuple-element.101), channel_id=1, source_target_pairs={{0,17},{1,16},{2,19},{3,18},{4,21},{5,20},{6,23},{7,22},{8,25},{9,... | collective-permute-start | bytes 835592 | tf_op jit(solution)/shard_map/ppermute | solution.py:697
  134.3 15.9 %collective-permute-start.12 = (bf16[4,1040,512]{2,1,0:T(8,128)(2,1)}, bf16[4,1040,512]{2,1,0:T(8,128)(2,1)S(1)}, u32[]{:S(2)}, u32[]{:S(2)}) collective-permute-start(bf16[4,1040,512]{2,1,0:T(8,128)(2,1)} %pass.4.refs_0_), channel_id=1, source_target_pairs={{0,8},{8,0},{16,24},{24,16},{1,9},{9,1},{17,25},{25,17},{2,10},{10... | collective-permute-start | bytes 12779528 | tf_op jit(solution)/shard_map/ppermute | solution.py:691
  134.4 7.1 %collective-permute-start.6 = (bf16[80,512]{1,0:T(8,128)(2,1)S(1)}, bf16[80,512]{1,0:T(8,128)(2,1)S(1)}, u32[]{:S(2)}, u32[]{:S(2)}) collective-permute-start(bf16[80,512]{1,0:T(8,128)(2,1)S(1)} %get-tuple-element.105), channel_id=1, source_target_pairs={{0,2},{1,3},{2,0},{3,1},{4,6},{5,7},{6,4},{7,5},{8,10},{9,11},{10,... | collective-permute-start | bytes 245768 | tf_op jit(solution)/shard_map/ppermute | solution.py:693
  136.1 9.6 %collective-permute-start.7 = (bf16[80,512]{1,0:T(8,128)(2,1)S(1)}, bf16[80,512]{1,0:T(8,128)(2,1)S(1)}, u32[]{:S(2)}, u32[]{:S(2)}) collective-permute-start(bf16[80,512]{1,0:T(8,128)(2,1)S(1)} %get-tuple-element.106), channel_id=1, source_target_pairs={{0,4},{1,5},{2,6},{3,7},{4,0},{5,1},{6,2},{7,3},{8,12},{9,13},{10,... | collective-permute-start | bytes 245768 | tf_op jit(solution)/shard_map/ppermute | solution.py:693
  138.5 7.2 %collective-permute-start.8 = (bf16[80,512]{1,0:T(8,128)(2,1)S(1)}, bf16[80,512]{1,0:T(8,128)(2,1)S(1)}, u32[]{:S(2)}, u32[]{:S(2)}) collective-permute-start(bf16[80,512]{1,0:T(8,128)(2,1)S(1)} %get-tuple-element.107), channel_id=1, source_target_pairs={{0,6},{1,7},{2,4},{3,5},{4,2},{5,3},{6,0},{7,1},{8,14},{9,15},{10,... | collective-permute-start | bytes 245768 | tf_op jit(solution)/shard_map/ppermute | solution.py:693
  145.8 7.8 %collective-permute-start.9 = (bf16[64,512]{1,0:T(8,128)(2,1)S(1)}, bf16[64,512]{1,0:T(8,128)(2,1)S(1)}, u32[]{:S(2)}, u32[]{:S(2)}) collective-permute-start(bf16[64,512]{1,0:T(8,128)(2,1)S(1)} %get-tuple-element.108.refs_2_.refs_0_), channel_id=1, source_target_pairs={{0,2},{1,3},{2,0},{3,1},{4,6},{5,7},{6,4},{7,5},{8,10},{9,11},{10,... | collective-permute-start | bytes 196616 | tf_op jit(solution)/shard_map/ppermute | solution.py:693
  147.5 7.6 %collective-permute-start.10 = (bf16[64,512]{1,0:T(8,128)(2,1)S(1)}, bf16[64,512]{1,0:T(8,128)(2,1)S(1)}, u32[]{:S(2)}, u32[]{:S(2)}) collective-permute-start(bf16[64,512]{1,0:T(8,128)(2,1)S(1)} %get-tuple-element.108.refs_2_.refs_0_), channel_id=1, source_target_pairs={{0,4},{1,5},{2,6},{3,7},{4,0},{5,1},{6,2},{7,3},{8,12},{9,13},{10,... | collective-permute-start | bytes 196616 | tf_op jit(solution)/shard_map/ppermute | solution.py:693
  148.9 6.2 %collective-permute-start.11 = (bf16[64,512]{1,0:T(8,128)(2,1)S(1)}, bf16[64,512]{1,0:T(8,128)(2,1)S(1)}, u32[]{:S(2)}, u32[]{:S(2)}) collective-permute-start(bf16[64,512]{1,0:T(8,128)(2,1)S(1)} %get-tuple-element.108.refs_2_.refs_0_), channel_id=1, source_target_pairs={{0,6},{1,7},{2,4},{3,5},{4,2},{5,3},{6,0},{7,1},{8,14},{9,15},{10,... | collective-permute-start | bytes 196616 | tf_op jit(solution)/shard_map/ppermute | solution.py:693
  155.1 8.7 %collective-permute-start.13 = (bf16[256,512]{1,0:T(8,128)(2,1)S(1)}, bf16[256,512]{1,0:T(8,128)(2,1)S(1)}, u32[]{:S(2)}, u32[]{:S(2)}) collective-permute-start(bf16[256,512]{1,0:T(8,128)(2,1)S(1)} %gather.1.refs_6_.refs_1_), channel_id=1, source_target_pairs={{0,1},{1,0},{2,3},{3,2},{4,5},{5,4},{6,7},{7,6},{8,9},{9,8},{10,11... | collective-permute-start | bytes 786440 | tf_op jit(solution)/shard_map/ppermute | solution.py:693
  156.6 8.7 %collective-permute-start.14 = (bf16[256,512]{1,0:T(8,128)(2,1)S(1)}, bf16[256,512]{1,0:T(8,128)(2,1)S(1)}, u32[]{:S(2)}, u32[]{:S(2)}) collective-permute-start(bf16[256,512]{1,0:T(8,128)(2,1)S(1)} %gather.1.refs_6_.refs_1_), channel_id=1, source_target_pairs={{0,16},{8,24},{16,0},{24,8},{1,17},{9,25},{17,1},{25,9},{2,18},{10... | collective-permute-start | bytes 786440 | tf_op jit(solution)/shard_map/ppermute | solution.py:691
  157.2 11.0 %collective-permute-start.15 = (bf16[256,512]{1,0:T(8,128)(2,1)S(1)}, bf16[256,512]{1,0:T(8,128)(2,1)S(1)}, u32[]{:S(2)}, u32[]{:S(2)}) collective-permute-start(bf16[256,512]{1,0:T(8,128)(2,1)S(1)} %gather.1.refs_6_.refs_1_), channel_id=1, source_target_pairs={{0,17},{1,16},{2,19},{3,18},{4,21},{5,20},{6,23},{7,22},{8,25},{9,... | collective-permute-start | bytes 786440 | tf_op jit(solution)/shard_map/ppermute | solution.py:697
  158.7 9.6 %collective-permute-start.16 = (bf16[256,512]{1,0:T(8,128)(2,1)S(1)}, bf16[256,512]{1,0:T(8,128)(2,1)S(1)}, u32[]{:S(2)}, u32[]{:S(2)}) collective-permute-start(bf16[256,512]{1,0:T(8,128)(2,1)S(1)} %gather.1.refs_6_.refs_1_), channel_id=1, source_target_pairs={{0,8},{8,0},{16,24},{24,16},{1,9},{9,1},{17,25},{25,17},{2,10},{10... | collective-permute-start | bytes 786440 | tf_op jit(solution)/shard_map/ppermute | solution.py:691
  163.8 4.4 %collective-permute-start.17 = (bf16[256,512]{1,0:T(8,128)(2,1)S(1)}, bf16[256,512]{1,0:T(8,128)(2,1)S(1)}, u32[]{:S(2)}, u32[]{:S(2)}) collective-permute-start(bf16[256,512]{1,0:T(8,128)(2,1)S(1)} %collective-permute-done.13.refs_2_), channel_id=1, source_target_pairs={{0,8},{8,0},{16,24},{24,16},{1,9},{9,1},{17,25},{25,17},{2,10},{10... | collective-permute-start | bytes 786440 | tf_op jit(solution)/shard_map/ppermute | solution.py:691
  165.4 2.9 %collective-permute-start.18 = (bf16[256,512]{1,0:T(8,128)(2,1)S(1)}, bf16[256,512]{1,0:T(8,128)(2,1)S(1)}, u32[]{:S(2)}, u32[]{:S(2)}) collective-permute-start(bf16[256,512]{1,0:T(8,128)(2,1)S(1)} %collective-permute-done.14.refs_3_), channel_id=1, source_target_pairs={{0,8},{8,0},{16,24},{24,16},{1,9},{9,1},{17,25},{25,17},{2,10},{10... | collective-permute-start | bytes 786440 | tf_op jit(solution)/shard_map/ppermute | solution.py:691
  168.2 1.5 collective-permute-start.19
  (3 other events, 53.1 us)
where the time goes:
time: 173 us
  Pallas kernels  90.6 us (52%)
  starting transfers between devices  40.9 us (24%)
  waiting for transfers between devices  39.7 us (23%)
    pallas_call x16, Pallas kernels, run(): pl.pallas_call(body, grid=grid, in_specs=list(in_specs) + [loose(value) f...  45.9 us
    pallas_call x5, Pallas kernels, fuse(): pl.pallas_call(body, in_specs=[spec(a) for a in args] + [loose(value) for...  44.7 us
    all_to_all x4, waiting for transfers between devices, exchange(): lax.all_to_all(value, 'wide', split_axis=0, concat_axis=0, tiled=True)  23 us
    all_to_all x4, starting transfers between devices, exchange(): lax.all_to_all(value, 'wide', split_axis=0, concat_axis=0, tiled=True)  21.5 us
    ppermute x8, starting transfers between devices, hop(): lax.ppermute(value, 'wide', [(i, i ^ wide_bits) for i in range(wide)])  12.5 us
    ppermute x8, waiting for transfers between devices, hop(): lax.ppermute(value, 'wide', [(i, i ^ wide_bits) for i in range(wide)])  7.46 us
    ppermute x10, waiting for transfers between devices, hop(): lax.ppermute(value, 'narrow', [(i, i ^ narrow_bits) for i in range(narrow)])  5.88 us
    ppermute x10, starting transfers between devices, hop(): lax.ppermute(value, 'narrow', [(i, i ^ narrow_bits) for i in range(narrow)])  4.34 us
  transfers between devices with their start and end apart: 24, of which 10 were waited for; matrix products, arithmetic and copies ran while one was open for 0% of the time, Pallas kernels for 41%

commit v1 on v0

--- a/solution.py
+++ b/solution.py
@@ -333,19 +333,14 @@
 
 
 def forward_kernel(experts, tile, me_ref, rows_ref, router_ref, up_bias_ref, *refs):
-    ups = refs[:-5]
-    hidden_ref, slope_ref, gate_ref, gates_ref, inner_s = refs[-5:]
+    ups = refs[:-4]
+    hidden_ref, slope_ref, gate_ref, gates_ref = refs[-4:]
     total = rows_ref.shape[0]
-    chunk = 16
+    chunk = total // 4
     root = math.sqrt(2.0 / math.pi)
-
-    def project(step):
-        inner_s[step % 2] = dot(rows_ref[...], ups[step][...])
-
+    rows = rows_ref[...]
     lane = lax.broadcasted_iota(jnp.int32, (total, LANES), 1)
-    logits = dot_nt(rows_ref[...], router_ref[...])
-    project(0)
-    logits = jnp.where(lane < experts, logits, -1e30)
+    logits = jnp.where(lane < experts, dot_nt(rows, router_ref[...]), -1e30)
     powers = jnp.exp(logits - jnp.max(logits, axis=-1, keepdims=True))
     gates = powers / jnp.sum(powers, axis=-1, keepdims=True)
     gates_ref[...] = gates
@@ -353,14 +348,11 @@
     gate = jnp.sum(jnp.where(lane == me_ref[0], gates, 0.0), axis=-1, keepdims=True)
     gate_ref[...] = jnp.broadcast_to(gate, (total, LANES))
     gate_ref.flush()
-    for step in range(len(ups)):
-        if step + 1 < len(ups):
-            project(step + 1)
+    for step, up_ref in enumerate(ups):
         lanes = slice(step * tile, (step + 1) * tile)
-        bias = up_bias_ref[:, lanes]
         for start in range(0, total, chunk):
             at = slice(start, start + chunk)
-            inner = inner_s[step % 2, at, :] + bias
+            inner = dot(rows[at], up_ref[...]) + up_bias_ref[:, lanes]
             square = inner * inner
             half = 0.5 + 0.5 * jnp.tanh(inner * (root + (root * 0.044715) * square))
             hidden = inner * half
@@ -424,9 +416,8 @@
     groups, refs = [refs[at * 5 : at * 5 + 5] for at in range(sets)], refs[5 * sets :]
     earlier, refs = refs[:again], refs[again:]
     extra_ref, out_ref, refs = refs[0], refs[1], refs[2:]
-    router_refs, gated_s, inner_grad_s, back_s = refs[:-3], refs[-3], refs[-2], refs[-1]
+    router_refs, gated_s, inner_grad_s = refs[:-2], refs[-2], refs[-1]
     total, width = groups[0][0].shape
-    chunk = 16
 
     @pl.when(pl.program_id(0) == 0)
     def _():
@@ -436,22 +427,18 @@
         if router_refs:
             router_refs[0][...] = dot_tn(extra_ref[...], groups[0][0][...])[: router_refs[0].shape[0]]
 
-    ones = jnp.ones((16, total), BF16)
     ups, downs, up_biases, down_biases = [], [], [], []
     for at, (rows_ref, grad_ref, gate_ref, hidden_ref, inner_grad_ref) in enumerate(groups):
         if again:
             slope_ref, inner_grad_ref = inner_grad_ref, inner_grad_s
-            back_s[...] = dot_nt(grad_ref[...], extra_ref[...])
-            for start in range(0, total, chunk):
-                here = slice(start, start + chunk)
-                gate = jnp.concatenate([gate_ref[here, :]] * (width // LANES), axis=1)
-                made = back_s[here, :] * gate * slope_ref[here, :].astype(F32)
-                inner_grad_s[here, :] = made.astype(BF16)
+            gate = jnp.concatenate([gate_ref[...]] * (width // LANES), axis=1)
+            made = dot_nt(grad_ref[...], extra_ref[...]) * gate * slope_ref[...].astype(F32)
+            inner_grad_s[...] = made.astype(BF16)
         inner_grad = inner_grad_ref[...]
         ups.append(dot_tn(rows_ref[...], inner_grad))
         downs.append(dot_tn(hidden_ref[...], gated_s[at]))
-        up_biases.append(dot(ones, inner_grad))
-        down_biases.append(dot(ones, gated_s[at]))
+        up_biases.append(jnp.sum(inner_grad.astype(F32), axis=0, keepdims=True))
+        down_biases.append(jnp.sum(gated_s[at].astype(F32), axis=0, keepdims=True))
 
     def put(some, parts):
         made = sum(parts[1:], parts[0]).astype(BF16)
@@ -782,7 +769,6 @@
                 32,
                 us,
                 "forward",
-                (pltpu.VMEM((2, slots_all, tile), F32),),
                 after=after,
             )
 
@@ -866,7 +852,6 @@
                 (
                     pltpu.VMEM((len(sets), slots_all, width), BF16),
                     pltpu.VMEM((slots_all, tile), BF16),
-                    pltpu.VMEM((slots_all, tile), F32),
                 ),
                 grid=(steps,),
                 in_specs=(

time: 173 us -> 172 us (level)
  Pallas kernels: 90.6 us -> 88.3 us
  waiting for transfers between devices: 39.7 us -> 41.8 us
    all_to_all x4, waiting for transfers between devices: 23 us -> 24.7 us  [exchange(): lax.all_to_all(value, 'wide', split_axis=0, concat_axis=0, tiled=True)]
  transfers between devices with their start and end apart: 24 -> 24, of which waited for: 10 -> 11; matrix products, arithmetic and copies ran while one was open for 0% -> 0% of each run, Pallas kernels for 41% -> 40%
where the time goes in v1:
time: 172 us; the launch traced here: 171 us
  Pallas kernels  88.3 us (51%)
  waiting for transfers between devices  41.8 us (24%)
  starting transfers between devices  39.8 us (23%)
    pallas_call x16, Pallas kernels, run(): pl.pallas_call(body, grid=grid, in_specs=list(in_specs) + [loose(value) f...  45 us
    pallas_call x5, Pallas kernels, fuse(): pl.pallas_call(body, in_specs=[spec(a) for a in args] + [loose(value) for...  43.3 us
    all_to_all x4, waiting for transfers between devices, exchange(): lax.all_to_all(value, 'wide', split_axis=0, concat_axis=0, tiled=True)  24.7 us
    all_to_all x4, starting transfers between devices, exchange(): lax.all_to_all(value, 'wide', split_axis=0, concat_axis=0, tiled=True)  20.5 us
    ppermute x8, starting transfers between devices, hop(): lax.ppermute(value, 'wide', [(i, i ^ wide_bits) for i in range(wide)])  12.5 us
    ppermute x8, waiting for transfers between devices, hop(): lax.ppermute(value, 'wide', [(i, i ^ wide_bits) for i in range(wide)])  7.47 us
    ppermute x10, waiting for transfers between devices, hop(): lax.ppermute(value, 'narrow', [(i, i ^ narrow_bits) for i in range(narrow)])  5.87 us
    ppermute x10, starting transfers between devices, hop(): lax.ppermute(value, 'narrow', [(i, i ^ narrow_bits) for i in range(narrow)])  4.31 us
  transfers between devices with their start and end apart: 24, of which 11 were waited for; matrix products, arithmetic and copies ran while one was open for 0% of the time, Pallas kernels for 40%

profile of v1, /device:TPU:0, one launch (start us, length us, event | category | flops | bytes accessed | tf_op | source)
XLA Modules:
  0.0 171.5 jit_solution(15862730824872781087)
XLA Ops:
  0.6 8.0 %attention.1 = (bf16[832,384]{1,0:T(8,128)(2,1)}, f32[384,8]{1,0:T(8,128)}, f32[8,128]{1,0:T(8,128)}, f32[384,512]{1,0:T(8,128)}, bf16[384,512]{1,0:T(8,128)(2,1...) custom-call(bf16[384,512]{1,0:T(8,128)(2,1)} %refs_16_.1, ...), custom_call_target="tpu_custom_call" | custom-call | flops 10000000000 | bytes 1000000 | tf_op jit(solution)/shard_map/attention/pallas_call | solution.py:176
  8.7 7.3 %all-to-all-start = ((bf16[8,104,512]{2,1,0:T(8,128)(2,1)}), bf16[8,104,512]{2,1,0:T(8,128)(2,1)S(1)}, u32[]{:S(2)}, u32[]{:S(2)}) async-start(bf16[8,104,512]{2,1,0:T(8,128)(2,1)} %bitcast.7), calls=%async_computation | async-start | bytes 1703936 | tf_op jit(solution)/shard_map/all_to_all | solution.py:725
  16.0 2.7 %dispatch.1 = bf16[832,512]{1,0:T(8,128)(2,1)} custom-call(bf16[832,384]{1,0:T(8,128)(2,1)} %get-tuple-element.78.refs_0_, bf16[384,512]{1,0:T(8,128)(2,1)} %refs_5_.3, bf16[832,512]{1,0:T(8,128)(2,1)} %get-tuple-element.74.refs_2_), custom_call_target="tpu_custom_call" | custom-call | flops 1000000000 | bytes 100000 | tf_op jit(solution)/shard_map/dispatch/pallas_call | solution.py:87
  18.7 18.9 %all-to-all-done = bf16[8,104,512]{2,1,0:T(8,128)(2,1)S(1)} async-done(((bf16[8,104,512]{2,1,0:T(8,128)(2,1)}), bf16[8,104,512]{2,1,0:T(8,128)(2,1)S(1)}, u32[]{:S(2)}, u32[]{:S(2)}) %all-to-all-start) | async-done | bytes 852000 | tf_op jit(solution)/shard_map/all_to_all | solution.py:725
  37.6 3.7 %all-to-all-start.1 = ((bf16[8,104,512]{2,1,0:T(8,128)(2,1)}), bf16[8,104,512]{2,1,0:T(8,128)(2,1)S(1)}, u32[]{:S(2)}, u32[]{:S(2)}) async-start(bf16[8,104,512]{2,1,0:T(8,128)(2,1)} %bitcast.59), calls=%async_computation.1 | async-start | bytes 1703936 | tf_op jit(solution)/shard_map/all_to_all | solution.py:725
  43.6 8.0 %forward.2 = (bf16[832,2048]{1,0:T(8,128)(2,1)}, bf16[832,2048]{1,0:T(8,128)(2,1)}, f32[832,128]{1,0:T(8,128)}, f32[832,128]{1,0:T(8,128)}) custom-call(s32[1]{0:T(128)} %bitcast.6.refs_0_, bf16[832,512]{1,0:T(8,128)(2,1)S(1)} %bitcast.35, bf16[128,512]{1,0:T(8,128)(2,1)} %pad.4.refs_2_.refs_8_, f32[1,2048]{1,0:T(1,128)} %refs_3_.3, ...), custom_call_target="tpu_custom_call" | custom-call | flops 10000000 | bytes 1000 | tf_op jit(solution)/shard_map/forward/pallas_call | solution.py:176
  51.6 6.6 %produce.1 = (bf16[832,512]{1,0:T(8,128)(2,1)}, bf16[832,512]{1,0:T(8,128)(2,1)}) custom-call(bf16[832,2048]{1,0:T(8,128)(2,1)} %get-tuple-element.75.refs_0_.refs_3_, bf16[2048,512]{1,0:T(8,128)(2,1)} %bitcast.50, f32[1,512]{1,0:T(1,128)} %refs_2_.1, f32[832,128]{1,0:T(8,128)} %get-tuple-element.76.refs_3_.refs_2_), custom_call_target="tpu_custom_call" | custom-call | flops 10000000 | bytes 1000 | tf_op jit(solution)/shard_map/produce/pallas_call | solution.py:87
  58.2 4.8 %all-to-all-done.1 = bf16[8,104,512]{2,1,0:T(8,128)(2,1)S(1)} async-done(((bf16[8,104,512]{2,1,0:T(8,128)(2,1)}), bf16[8,104,512]{2,1,0:T(8,128)(2,1)S(1)}, u32[]{:S(2)}, u32[]{:S(2)}) %all-to-all-start.1) | async-done | bytes 852000 | tf_op jit(solution)/shard_map/all_to_all | solution.py:725
  63.0 9.1 %experts.1 = (bf16[832,2048]{1,0:T(8,128)(2,1)}, bf16[832,512]{1,0:T(8,128)(2,1)}, bf16[832,128]{1,0:T(8,128)(2,1)}) custom-call(s32[1]{0:T(128)} %bitcast.6.refs_0_, bf16[832,512]{1,0:T(8,128)(2,1)S(1)} %bitcast.29, f32[832,128]{1,0:T(8,128)} %get-tuple-element.76.refs_3_.refs_2_, bf16[2048,512]{1,0:T(8,128)(2,1)} %bitcast.51, ...), custom_call_target="tpu_custom_call" | custom-call | flops 10000000 | bytes 1000 | tf_op jit(solution)/shard_map/experts/pallas_call | solution.py:176
  72.1 4.5 %all-to-all-start.3 = ((bf16[8,104,512]{2,1,0:T(8,128)(2,1)}), bf16[8,104,512]{2,1,0:T(8,128)(2,1)S(1)}, u32[]{:S(2)}, u32[]{:S(2)}) async-start(bf16[8,104,512]{2,1,0:T(8,128)(2,1)} %bitcast.17), calls=%async_computation.3 | async-start | bytes 1703936 | tf_op jit(solution)/shard_map/all_to_all | solution.py:725
  79.2 8.4 %forward.3 = (bf16[832,2048]{1,0:T(8,128)(2,1)}, bf16[832,2048]{1,0:T(8,128)(2,1)}, f32[832,128]{1,0:T(8,128)}, f32[832,128]{1,0:T(8,128)}) custom-call(s32[1]{0:T(128)} %bitcast.6.refs_0_, bf16[832,512]{1,0:T(8,128)(2,1)} %copy-done, bf16[128,512]{1,0:T(8,128)(2,1)} %pad.4.refs_2_.refs_8_, f32[1,2048]{1,0:T(1,128)} %refs_3_.3, bf16[512,2048]{1,0:T(8,128)(2,1)} %bitcast.46, ...), custom_call_target="tpu_custom_call" | custom-call | flops 10000000 | bytes 1000 | tf_op jit(solution)/shard_map/forward/pallas_call | solution.py:176
  87.5 9.0 %expert_weights.2 = (bf16[4,1040,512]{2,1,0:T(8,128)(2,1)}, f32[8,512]{1,0:T(8,128)}) custom-call(bf16[832,512]{1,0:T(8,128)(2,1)S(1)} %bitcast.36, bf16[832,512]{1,0:T(8,128)(2,1)S(1)} %bitcast.31, f32[832,128]{1,0:T(8,128)} %get-tuple-element.76.refs_3_.refs_2_, bf16[832,2048]{1,0:T(8,128)(2,1)} %get-tuple-element.75.refs_0_.refs_3_, ...), custom_call_target="tpu_custom_call" | custom-call | flops 10000000 | bytes 1000 | tf_op jit(solution)/shard_map/expert_weights/pallas_call | solution.py:87
  97.6 5.0 %all-to-all-start.2 = ((bf16[8,104,512]{2,1,0:T(8,128)(2,1)}), bf16[8,104,512]{2,1,0:T(8,128)(2,1)S(1)}, u32[]{:S(2)}, u32[]{:S(2)}) async-start(bf16[8,104,512]{2,1,0:T(8,128)(2,1)} %bitcast.58), calls=%async_computation.2 | async-start | bytes 1703936 | tf_op jit(solution)/shard_map/all_to_all | solution.py:725
  102.5 9.7 %backward.1 = (bf16[1040,512]{1,0:T(8,128)(2,1)}, bf16[1040,512]{1,0:T(8,128)(2,1)}, bf16[384,512]{1,0:T(8,128)(2,1)}) custom-call(s32[1]{0:T(128)} %bitcast.16.refs_0_, bf16[832,512]{1,0:T(8,128)(2,1)S(1)} %bitcast.37, f32[384,8]{1,0:T(8,128)} %get-tuple-element.72.refs_0_.refs_2_, f32[384,512]{1,0:T(8,128)} %get-tuple-element.73.refs_1_.refs_3_, ...), custom_call_target="tpu_custom_call" | custom-call | flops 10000000 | bytes 1000 | tf_op jit(solution)/shard_map/backward/pallas_call | solution.py:176
  112.3 2.9 %collective-permute-done.2.refs_2_ = bf16[1040,512]{1,0:T(8,128)(2,1)S(1)} collective-permute-done((bf16[1040,512]{1,0:T(8,128)(2,1)}, bf16[1040,512]{1,0:T(8,128)(2,1)S(1)}, u32[]{:S(2)}, u32[]{:S(2)}) %collective-permute-start.2) | collective-permute-done | bytes 1064992 | tf_op jit(solution)/shard_map/ppermute | solution.py:678
  116.7 2.1 %collective-permute-start.3 = (bf16[272,512]{1,0:T(8,128)(2,1)S(1)}, bf16[272,512]{1,0:T(8,128)(2,1)S(1)}, u32[]{:S(2)}, u32[]{:S(2)}) collective-permute-start(bf16[272,512]{1,0:T(8,128)(2,1)S(1)} %get-tuple-element.99), channel_id=1, source_target_pairs={{0,1},{1,0},{2,3},{3,2},{4,5},{5,4},{6,7},{7,6},{8,9},{9,8},{10,11... | collective-permute-start | bytes 835592 | tf_op jit(solution)/shard_map/ppermute | solution.py:680
  120.3 11.7 %expert_weights.3.refs_5_.refs_0_ = bf16[4,1040,512]{2,1,0:T(8,128)(2,1)} custom-call(bf16[832,512]{1,0:T(8,128)(2,1)} %copy-done, bf16[832,512]{1,0:T(8,128)(2,1)} %copy-done.1, f32[832,128]{1,0:T(8,128)} %get-tuple-element.102.refs_2_, bf16[832,2048]{1,0:T(8,128)(2,1)} %get-tuple-element.103.refs_3_, bf16[832,2048]{1,0:T(8,128)(2,1)} %get-tuple-element.84.refs_6_.refs_4_, ...), custom_call_target="tpu_custom_call" | custom-call | flops 10000000 | bytes 1000 | tf_op jit(solution)/shard_map/expert_weights/pallas_call | solution.py:87
  134.9 2.4 %collective-permute-start.7 = (bf16[80,512]{1,0:T(8,128)(2,1)S(1)}, bf16[80,512]{1,0:T(8,128)(2,1)S(1)}, u32[]{:S(2)}, u32[]{:S(2)}) collective-permute-start(bf16[80,512]{1,0:T(8,128)(2,1)S(1)} %get-tuple-element.106), channel_id=1, source_target_pairs={{0,4},{1,5},{2,6},{3,7},{4,0},{5,1},{6,2},{7,3},{8,12},{9,13},{10,... | collective-permute-start | bytes 245768 | tf_op jit(solution)/shard_map/ppermute | solution.py:680
  137.6 2.6 %combine.1.refs_4_ = bf16[384,512]{1,0:T(8,128)(2,1)} custom-call(f32[384,8]{1,0:T(8,128)} %get-tuple-element.72.refs_0_.refs_2_, f32[384,512]{1,0:T(8,128)} %get-tuple-element.73.refs_1_.refs_3_, bf16[832,512]{1,0:T(8,128)(2,1)S(1)} %bitcast.33), custom_call_target="tpu_custom_call" | custom-call | flops 10000000 | bytes 1000 | tf_op jit(solution)/shard_map/combine/pallas_call | solution.py:87
  140.3 4.2 %collective-permute-done.7.refs_2_ = bf16[80,512]{1,0:T(8,128)(2,1)S(1)} collective-permute-done((bf16[80,512]{1,0:T(8,128)(2,1)S(1)}, bf16[80,512]{1,0:T(8,128)(2,1)S(1)}, u32[]{:S(2)}, u32[]{:S(2)}) %collective-permute-start.7) | collective-permute-done | bytes 81952 | tf_op jit(solution)/shard_map/ppermute | solution.py:680
  149.0 3.4 %finish_experts.2 = (f32[512,2048]{1,0:T(8,128)}, f32[1,2048]{1,0:T(1,128)}, f32[2048,512]{1,0:T(8,128)}, f32[1,512]{1,0:T(1,128)}) custom-call(bf16[4,1040,512]{2,1,0:T(8,128)(2,1)} %pass.4.refs_0_, bf16[4,1040,512]{2,1,0:T(8,128)(2,1)S(1)} %collective-permute-done.12.refs_1_, bf16[64,512]{1,0:T(8,128)(2,1)S(1)} %get-tuple-element.108.refs_2_.refs_0_), custom_call_target="tpu_custom_call" | custom-call | flops 10000000 | bytes 1000 | tf_op jit(solution)/shard_map/finish_experts/pallas_call | solution.py:87
  157.5 3.4 %finish_experts.3 = (f32[512,2048]{1,0:T(8,128)}, f32[1,2048]{1,0:T(1,128)}, f32[2048,512]{1,0:T(8,128)}, f32[1,512]{1,0:T(1,128)}) custom-call(bf16[4,1040,512]{2,1,0:T(8,128)(2,1)} %pass.4.refs_0_, bf16[4,1040,512]{2,1,0:T(8,128)(2,1)S(1)} %collective-permute-done.12.refs_1_, ...), custom_call_target="tpu_custom_call", output_to_operand_aliasing={{0}: (2, {}), {1}: (3, {}), {2}: (4, {}), {3}: (5, {})} | custom-call | flops 10000000 | bytes 1000 | tf_op jit(solution)/shard_map/finish_experts/pallas_call | solution.py:87
  164.2 2.8 %collective-permute-done.15.refs_0_ = bf16[256,512]{1,0:T(8,128)(2,1)S(1)} collective-permute-done((bf16[256,512]{1,0:T(8,128)(2,1)S(1)}, bf16[256,512]{1,0:T(8,128)(2,1)S(1)}, u32[]{:S(2)}, u32[]{:S(2)}) %collective-permute-start.15) | collective-permute-done | bytes 262176 | tf_op jit(solution)/shard_map/ppermute | solution.py:684
  168.5 3.0 %finish_shared.1 = (f32[512,512]{1,0:T(8,128)}, f32[512,512]{1,0:T(8,128)}, f32[512,512]{1,0:T(8,128)}, f32[512,512]{1,0:T(8,128)}, f32[1,512]{1,0:T(1,128)}, /*...) custom-call(s32[3]{0:T(128)S(1)} %pad_add_fusion.refs_0_, ...), custom_call_target="tpu_custom_call" | custom-call | flops 3000000000 | bytes 300000 | tf_op jit(solution)/shard_map/finish_shared/pallas_call | solution.py:87
  (53 shorter events, 26.6 us)
Async XLA Ops:
  8.7 28.9 %all-to-all-start = ((bf16[8,104,512]{2,1,0:T(8,128)(2,1)}), bf16[8,104,512]{2,1,0:T(8,128)(2,1)S(1)}, u32[]{:S(2)}, u32[]{:S(2)}) async-start(bf16[8,104,512]{2,1,0:T(8,128)(2,1)} %bitcast.7), calls=%async_computation | async-start | bytes 1703936 | tf_op jit(solution)/shard_map/all_to_all | solution.py:725
  37.6 25.3 %all-to-all-start.1 = ((bf16[8,104,512]{2,1,0:T(8,128)(2,1)}), bf16[8,104,512]{2,1,0:T(8,128)(2,1)S(1)}, u32[]{:S(2)}, u32[]{:S(2)}) async-start(bf16[8,104,512]{2,1,0:T(8,128)(2,1)} %bitcast.59), calls=%async_computation.1 | async-start | bytes 1703936 | tf_op jit(solution)/shard_map/all_to_all | solution.py:725
  41.4 21.6 %collective-permute-start = (bf16[832,512]{1,0:T(8,128)(2,1)S(1)}, bf16[832,512]{1,0:T(8,128)(2,1)S(1)}, u32[]{:S(2)}, u32[]{:S(2)}) collective-permute-start(bf16[832,512]{1,0:T(8,128)(2,1)S(1)} %bitcast.34), channel_id=1, source_target_pairs={{0,16},{8,24},{16,0},{24,8},{1,17},{9,25},{17,1},{25,9},{2,18},{10... | collective-permute-start | bytes 2555912 | tf_op jit(solution)/shard_map/ppermute | solution.py:678
  72.1 25.4 %all-to-all-start.3 = ((bf16[8,104,512]{2,1,0:T(8,128)(2,1)}), bf16[8,104,512]{2,1,0:T(8,128)(2,1)S(1)}, u32[]{:S(2)}, u32[]{:S(2)}) async-start(bf16[8,104,512]{2,1,0:T(8,128)(2,1)} %bitcast.17), calls=%async_computation.3 | async-start | bytes 1703936 | tf_op jit(solution)/shard_map/all_to_all | solution.py:725
  77.6 24.9 %collective-permute-start.1 = (bf16[832,512]{1,0:T(8,128)(2,1)}, bf16[832,512]{1,0:T(8,128)(2,1)S(1)}, u32[]{:S(2)}, u32[]{:S(2)}) collective-permute-start(bf16[832,512]{1,0:T(8,128)(2,1)} %copy_rows.1), channel_id=1, source_target_pairs={{0,16},{8,24},{16,0},{24,8},{1,17},{9,25},{17,1},{25,9},{2,18},{10... | collective-permute-start | bytes 2555912 | tf_op jit(solution)/shard_map/ppermute | solution.py:678
  97.6 34.5 %all-to-all-start.2 = ((bf16[8,104,512]{2,1,0:T(8,128)(2,1)}), bf16[8,104,512]{2,1,0:T(8,128)(2,1)S(1)}, u32[]{:S(2)}, u32[]{:S(2)}) async-start(bf16[8,104,512]{2,1,0:T(8,128)(2,1)} %bitcast.58), calls=%async_computation.2 | async-start | bytes 1703936 | tf_op jit(solution)/shard_map/all_to_all | solution.py:725
  112.2 3.0 %collective-permute-start.2 = (bf16[1040,512]{1,0:T(8,128)(2,1)}, bf16[1040,512]{1,0:T(8,128)(2,1)S(1)}, u32[]{:S(2)}, u32[]{:S(2)}) collective-permute-start(bf16[1040,512]{1,0:T(8,128)(2,1)} %get-tuple-element.97), channel_id=1, source_target_pairs={{0,8},{8,0},{16,24},{24,16},{1,9},{9,1},{17,25},{25,17},{2,10},{10... | collective-permute-start | bytes 3194888 | tf_op jit(solution)/shard_map/ppermute | solution.py:678
  116.7 15.3 %collective-permute-start.3 = (bf16[272,512]{1,0:T(8,128)(2,1)S(1)}, bf16[272,512]{1,0:T(8,128)(2,1)S(1)}, u32[]{:S(2)}, u32[]{:S(2)}) collective-permute-start(bf16[272,512]{1,0:T(8,128)(2,1)S(1)} %get-tuple-element.99), channel_id=1, source_target_pairs={{0,1},{1,0},{2,3},{3,2},{4,5},{5,4},{6,7},{7,6},{8,9},{9,8},{10,11... | collective-permute-start | bytes 835592 | tf_op jit(solution)/shard_map/ppermute | solution.py:680
  118.8 13.2 %collective-permute-start.4 = (bf16[272,512]{1,0:T(8,128)(2,1)S(1)}, bf16[272,512]{1,0:T(8,128)(2,1)S(1)}, u32[]{:S(2)}, u32[]{:S(2)}) collective-permute-start(bf16[272,512]{1,0:T(8,128)(2,1)S(1)} %get-tuple-element.100), channel_id=1, source_target_pairs={{0,16},{8,24},{16,0},{24,8},{1,17},{9,25},{17,1},{25,9},{2,18},{10... | collective-permute-start | bytes 835592 | tf_op jit(solution)/shard_map/ppermute | solution.py:678
  119.3 13.7 %collective-permute-start.5 = (bf16[272,512]{1,0:T(8,128)(2,1)S(1)}, bf16[272,512]{1,0:T(8,128)(2,1)S(1)}, u32[]{:S(2)}, u32[]{:S(2)}) collective-permute-start(bf16[272,512]{1,0:T(8,128)(2,1)S(1)} %get-tuple-element.101), channel_id=1, source_target_pairs={{0,17},{1,16},{2,19},{3,18},{4,21},{5,20},{6,23},{7,22},{8,25},{9,... | collective-permute-start | bytes 835592 | tf_op jit(solution)/shard_map/ppermute | solution.py:684
  133.1 15.9 %collective-permute-start.12 = (bf16[4,1040,512]{2,1,0:T(8,128)(2,1)}, bf16[4,1040,512]{2,1,0:T(8,128)(2,1)S(1)}, u32[]{:S(2)}, u32[]{:S(2)}) collective-permute-start(bf16[4,1040,512]{2,1,0:T(8,128)(2,1)} %pass.4.refs_0_), channel_id=1, source_target_pairs={{0,8},{8,0},{16,24},{24,16},{1,9},{9,1},{17,25},{25,17},{2,10},{10... | collective-permute-start | bytes 12779528 | tf_op jit(solution)/shard_map/ppermute | solution.py:678
  133.2 7.1 %collective-permute-start.6 = (bf16[80,512]{1,0:T(8,128)(2,1)S(1)}, bf16[80,512]{1,0:T(8,128)(2,1)S(1)}, u32[]{:S(2)}, u32[]{:S(2)}) collective-permute-start(bf16[80,512]{1,0:T(8,128)(2,1)S(1)} %get-tuple-element.105), channel_id=1, source_target_pairs={{0,2},{1,3},{2,0},{3,1},{4,6},{5,7},{6,4},{7,5},{8,10},{9,11},{10,... | collective-permute-start | bytes 245768 | tf_op jit(solution)/shard_map/ppermute | solution.py:680
  134.9 9.6 %collective-permute-start.7 = (bf16[80,512]{1,0:T(8,128)(2,1)S(1)}, bf16[80,512]{1,0:T(8,128)(2,1)S(1)}, u32[]{:S(2)}, u32[]{:S(2)}) collective-permute-start(bf16[80,512]{1,0:T(8,128)(2,1)S(1)} %get-tuple-element.106), channel_id=1, source_target_pairs={{0,4},{1,5},{2,6},{3,7},{4,0},{5,1},{6,2},{7,3},{8,12},{9,13},{10,... | collective-permute-start | bytes 245768 | tf_op jit(solution)/shard_map/ppermute | solution.py:680
  137.3 7.2 %collective-permute-start.8 = (bf16[80,512]{1,0:T(8,128)(2,1)S(1)}, bf16[80,512]{1,0:T(8,128)(2,1)S(1)}, u32[]{:S(2)}, u32[]{:S(2)}) collective-permute-start(bf16[80,512]{1,0:T(8,128)(2,1)S(1)} %get-tuple-element.107), channel_id=1, source_target_pairs={{0,6},{1,7},{2,4},{3,5},{4,2},{5,3},{6,0},{7,1},{8,14},{9,15},{10,... | collective-permute-start | bytes 245768 | tf_op jit(solution)/shard_map/ppermute | solution.py:680
  144.5 7.8 %collective-permute-start.9 = (bf16[64,512]{1,0:T(8,128)(2,1)S(1)}, bf16[64,512]{1,0:T(8,128)(2,1)S(1)}, u32[]{:S(2)}, u32[]{:S(2)}) collective-permute-start(bf16[64,512]{1,0:T(8,128)(2,1)S(1)} %get-tuple-element.108.refs_2_.refs_0_), channel_id=1, source_target_pairs={{0,2},{1,3},{2,0},{3,1},{4,6},{5,7},{6,4},{7,5},{8,10},{9,11},{10,... | collective-permute-start | bytes 196616 | tf_op jit(solution)/shard_map/ppermute | solution.py:680
  146.3 7.6 %collective-permute-start.10 = (bf16[64,512]{1,0:T(8,128)(2,1)S(1)}, bf16[64,512]{1,0:T(8,128)(2,1)S(1)}, u32[]{:S(2)}, u32[]{:S(2)}) collective-permute-start(bf16[64,512]{1,0:T(8,128)(2,1)S(1)} %get-tuple-element.108.refs_2_.refs_0_), channel_id=1, source_target_pairs={{0,4},{1,5},{2,6},{3,7},{4,0},{5,1},{6,2},{7,3},{8,12},{9,13},{10,... | collective-permute-start | bytes 196616 | tf_op jit(solution)/shard_map/ppermute | solution.py:680
  147.7 6.2 %collective-permute-start.11 = (bf16[64,512]{1,0:T(8,128)(2,1)S(1)}, bf16[64,512]{1,0:T(8,128)(2,1)S(1)}, u32[]{:S(2)}, u32[]{:S(2)}) collective-permute-start(bf16[64,512]{1,0:T(8,128)(2,1)S(1)} %get-tuple-element.108.refs_2_.refs_0_), channel_id=1, source_target_pairs={{0,6},{1,7},{2,4},{3,5},{4,2},{5,3},{6,0},{7,1},{8,14},{9,15},{10,... | collective-permute-start | bytes 196616 | tf_op jit(solution)/shard_map/ppermute | solution.py:680
  153.9 8.7 %collective-permute-start.13 = (bf16[256,512]{1,0:T(8,128)(2,1)S(1)}, bf16[256,512]{1,0:T(8,128)(2,1)S(1)}, u32[]{:S(2)}, u32[]{:S(2)}) collective-permute-start(bf16[256,512]{1,0:T(8,128)(2,1)S(1)} %gather.1.refs_6_.refs_1_), channel_id=1, source_target_pairs={{0,1},{1,0},{2,3},{3,2},{4,5},{5,4},{6,7},{7,6},{8,9},{9,8},{10,11... | collective-permute-start | bytes 786440 | tf_op jit(solution)/shard_map/ppermute | solution.py:680
  155.4 8.7 %collective-permute-start.14 = (bf16[256,512]{1,0:T(8,128)(2,1)S(1)}, bf16[256,512]{1,0:T(8,128)(2,1)S(1)}, u32[]{:S(2)}, u32[]{:S(2)}) collective-permute-start(bf16[256,512]{1,0:T(8,128)(2,1)S(1)} %gather.1.refs_6_.refs_1_), channel_id=1, source_target_pairs={{0,16},{8,24},{16,0},{24,8},{1,17},{9,25},{17,1},{25,9},{2,18},{10... | collective-permute-start | bytes 786440 | tf_op jit(solution)/shard_map/ppermute | solution.py:678
  155.9 11.0 %collective-permute-start.15 = (bf16[256,512]{1,0:T(8,128)(2,1)S(1)}, bf16[256,512]{1,0:T(8,128)(2,1)S(1)}, u32[]{:S(2)}, u32[]{:S(2)}) collective-permute-start(bf16[256,512]{1,0:T(8,128)(2,1)S(1)} %gather.1.refs_6_.refs_1_), channel_id=1, source_target_pairs={{0,17},{1,16},{2,19},{3,18},{4,21},{5,20},{6,23},{7,22},{8,25},{9,... | collective-permute-start | bytes 786440 | tf_op jit(solution)/shard_map/ppermute | solution.py:684
  157.4 9.6 %collective-permute-start.16 = (bf16[256,512]{1,0:T(8,128)(2,1)S(1)}, bf16[256,512]{1,0:T(8,128)(2,1)S(1)}, u32[]{:S(2)}, u32[]{:S(2)}) collective-permute-start(bf16[256,512]{1,0:T(8,128)(2,1)S(1)} %gather.1.refs_6_.refs_1_), channel_id=1, source_target_pairs={{0,8},{8,0},{16,24},{24,16},{1,9},{9,1},{17,25},{25,17},{2,10},{10... | collective-permute-start | bytes 786440 | tf_op jit(solution)/shard_map/ppermute | solution.py:678
  162.6 4.4 %collective-permute-start.17 = (bf16[256,512]{1,0:T(8,128)(2,1)S(1)}, bf16[256,512]{1,0:T(8,128)(2,1)S(1)}, u32[]{:S(2)}, u32[]{:S(2)}) collective-permute-start(bf16[256,512]{1,0:T(8,128)(2,1)S(1)} %collective-permute-done.13.refs_2_), channel_id=1, source_target_pairs={{0,8},{8,0},{16,24},{24,16},{1,9},{9,1},{17,25},{25,17},{2,10},{10... | collective-permute-start | bytes 786440 | tf_op jit(solution)/shard_map/ppermute | solution.py:678
  164.2 2.9 %collective-permute-start.18 = (bf16[256,512]{1,0:T(8,128)(2,1)S(1)}, bf16[256,512]{1,0:T(8,128)(2,1)S(1)}, u32[]{:S(2)}, u32[]{:S(2)}) collective-permute-start(bf16[256,512]{1,0:T(8,128)(2,1)S(1)} %collective-permute-done.14.refs_3_), channel_id=1, source_target_pairs={{0,8},{8,0},{16,24},{24,16},{1,9},{9,1},{17,25},{25,17},{2,10},{10... | collective-permute-start | bytes 786440 | tf_op jit(solution)/shard_map/ppermute | solution.py:678
  167.0 1.5 collective-permute-start.19
  (3 other events, 53.1 us)

commit v2 on v1

--- a/solution.py
+++ b/solution.py
@@ -253,18 +253,17 @@
 def attention_kernel(
     capacity,
     experts,
+    picks_ref,
+    ranks_ref,
     tokens_ref,
     gain_one_ref,
     shift_one_ref,
-    picks_ref,
-    ranks_ref,
     query_w_ref,
     key_w_ref,
     value_w_ref,
     out_w_ref,
     gain_two_ref,
     shift_two_ref,
-    spread_ref,
     target_ref,
     count_ref,
     resid_ref,
@@ -275,16 +274,16 @@
     weight_ref,
     mixed_ref,
     sent_ref,
+    spread_ref,
 ):
     count, width = tokens_ref.shape
+    route(capacity, experts, picks_ref, ranks_ref, spread_ref, target_ref, count_ref)
+    target_ref.flush()
+    count_ref.flush()
     inputs = tokens_ref[...].astype(F32)
     hat, _ = norm_rows(inputs)
     normed_ref[...] = (hat * gain_one_ref[...] + shift_one_ref[...]).astype(BF16)
     normed_ref.flush()
-    route(capacity, experts, picks_ref, ranks_ref, spread_ref, target_ref, count_ref)
-    spread_ref.flush()
-    target_ref.flush()
-    count_ref.flush()
     normed = normed_ref[...]
     scale = 1.0 / math.sqrt(width // HEADS)
     query_ref[...] = (dot(normed, query_w_ref[...]).astype(BF16).astype(F32) * scale).astype(BF16)
@@ -300,7 +299,7 @@
     row_image = (lax.broadcasted_iota(jnp.int32, (2 * block, block), 0) % block) // PATCHES
     column_image = lax.broadcasted_iota(jnp.int32, (2 * block, block), 1) // PATCHES
     bias = jnp.where(row_image == column_image, 0.0, -1e30)
-    together = 8
+    together = 1
     cells = [(item, pair) for item in range(count // block) for pair in range(pairs)]
     for start in range(0, len(cells), together):
         work = []
@@ -328,8 +327,8 @@
     sent_ref[...] = dot(spread_ref[...], second).astype(BF16)
 
 
-def dispatch_kernel(spread_ref, second_ref, sent_ref):
-    sent_ref[...] = dot(spread_ref[...], second_ref[...]).astype(BF16)
+def dispatch_kernel(target_ref, given_ref, sent_ref):
+    sent_ref[...] = dot_tn(one_hot_rows(target_ref, sent_ref.shape[0]), given_ref[...]).astype(BF16)
 
 
 def forward_kernel(experts, tile, me_ref, rows_ref, router_ref, up_bias_ref, *refs):
@@ -728,11 +727,10 @@
         rows_shape = shape((slots_all, width), BF16)
         lanes_shape = shape((slots_all, LANES), F32)
         narrow_far = far((count, width), BF16)
-        spread, target, counts, resid, normed, queries, keys, values, weights, mixed, sent = fuse(
+        target, counts, resid, normed, queries, keys, values, weights, mixed, sent = fuse(
             functools.partial(attention_kernel, capacity, experts),
-            (tokens, gain_one, shift_one, picks.T, ranks.T, query_w, key_w, value_w, out_w, gain_two, shift_two),
+            (picks.T, ranks.T, tokens, gain_one, shift_one, query_w, key_w, value_w, out_w, gain_two, shift_two),
             (
-                far((slots_all, count), BF16),
                 far((count, 8), F32),
                 far((8, LANES), F32),
                 far((count, width), F32),
@@ -747,9 +745,10 @@
             32,
             10,
             "attention",
+            (pltpu.VMEM((slots_all, count), BF16),),
         )
         rows = exchange(sent)
-        (grad_sent,) = run(dispatch_kernel, (spread, out_grad), (rows_shape,), 16, 1, "dispatch", after=(Held(sent),))
+        (grad_sent,) = run(dispatch_kernel, (target, out_grad), (rows_shape,), 16, 1, "dispatch", after=(Held(sent),))
         grad_rows = exchange(grad_sent)
 
         whole = pl.BlockSpec((slots_all, width), lambda f: (0, 0))

time: 172 us -> 172 us (level)
  no operation moved by 1% of the time
where the time goes in v2:
time: 172 us; the launch traced here: 171 us
  Pallas kernels  87.8 us (51%)
  waiting for transfers between devices  41.7 us (24%)
  starting transfers between devices  39.8 us (23%)
    pallas_call x16, Pallas kernels, run(): pl.pallas_call(body, grid=grid, in_specs=list(in_specs) + [loose(value) f...  45.1 us
    pallas_call x5, Pallas kernels, fuse(): pl.pallas_call(body, in_specs=[spec(a) for a in args] + [loose(value) for...  42.7 us
    all_to_all x4, waiting for transfers between devices, exchange(): lax.all_to_all(value, 'wide', split_axis=0, concat_axis=0, tiled=True)  24.7 us
    all_to_all x4, starting transfers between devices, exchange(): lax.all_to_all(value, 'wide', split_axis=0, concat_axis=0, tiled=True)  20.4 us
    ppermute x8, starting transfers between devices, hop(): lax.ppermute(value, 'wide', [(i, i ^ wide_bits) for i in range(wide)])  12.5 us
    ppermute x8, waiting for transfers between devices, hop(): lax.ppermute(value, 'wide', [(i, i ^ wide_bits) for i in range(wide)])  7.47 us
    ppermute x10, waiting for transfers between devices, hop(): lax.ppermute(value, 'narrow', [(i, i ^ narrow_bits) for i in range(narrow)])  5.87 us
    ppermute x10, starting transfers between devices, hop(): lax.ppermute(value, 'narrow', [(i, i ^ narrow_bits) for i in range(narrow)])  4.34 us
  transfers between devices with their start and end apart: 24, of which 11 were waited for; matrix products, arithmetic and copies ran while one was open for 0% of the time, Pallas kernels for 40%

profile of v2, /device:TPU:0, one launch (start us, length us, event | category | flops | bytes accessed | tf_op | source)
XLA Modules:
  0.0 170.9 jit_solution(4407632214729332380)
XLA Ops:
  0.6 7.5 %attention.1 = (f32[384,8]{1,0:T(8,128)}, f32[8,128]{1,0:T(8,128)}, f32[384,512]{1,0:T(8,128)}, bf16[384,512]{1,0:T(8,128)(2,1)}, bf16[384,512]{1,0:T(8,128)(2,1...) custom-call(s32[2,384]{1,0:T(2,128)} %bitcast.65, ...), custom_call_target="tpu_custom_call" | custom-call | flops 10000000000 | bytes 1000000 | tf_op jit(solution)/shard_map/attention/pallas_call | solution.py:176
  8.1 7.3 %all-to-all-start = ((bf16[8,104,512]{2,1,0:T(8,128)(2,1)}), bf16[8,104,512]{2,1,0:T(8,128)(2,1)S(1)}, u32[]{:S(2)}, u32[]{:S(2)}) async-start(bf16[8,104,512]{2,1,0:T(8,128)(2,1)} %bitcast.7), calls=%async_computation | async-start | bytes 1703936 | tf_op jit(solution)/shard_map/all_to_all | solution.py:724
  15.4 2.8 %dispatch.1 = bf16[832,512]{1,0:T(8,128)(2,1)} custom-call(f32[384,8]{1,0:T(8,128)} %get-tuple-element.71.refs_0_.refs_2_, bf16[384,512]{1,0:T(8,128)(2,1)} %refs_5_.3, bf16[832,512]{1,0:T(8,128)(2,1)} %get-tuple-element.73.refs_2_), custom_call_target="tpu_custom_call" | custom-call | flops 1000000000 | bytes 100000 | tf_op jit(solution)/shard_map/dispatch/pallas_call | solution.py:87
  18.2 18.8 %all-to-all-done = bf16[8,104,512]{2,1,0:T(8,128)(2,1)S(1)} async-done(((bf16[8,104,512]{2,1,0:T(8,128)(2,1)}), bf16[8,104,512]{2,1,0:T(8,128)(2,1)S(1)}, u32[]{:S(2)}, u32[]{:S(2)}) %all-to-all-start) | async-done | bytes 852000 | tf_op jit(solution)/shard_map/all_to_all | solution.py:724
  37.1 3.7 %all-to-all-start.1 = ((bf16[8,104,512]{2,1,0:T(8,128)(2,1)}), bf16[8,104,512]{2,1,0:T(8,128)(2,1)S(1)}, u32[]{:S(2)}, u32[]{:S(2)}) async-start(bf16[8,104,512]{2,1,0:T(8,128)(2,1)} %bitcast.59), calls=%async_computation.1 | async-start | bytes 1703936 | tf_op jit(solution)/shard_map/all_to_all | solution.py:724
  43.0 8.1 %forward.2 = (bf16[832,2048]{1,0:T(8,128)(2,1)}, bf16[832,2048]{1,0:T(8,128)(2,1)}, f32[832,128]{1,0:T(8,128)}, f32[832,128]{1,0:T(8,128)}) custom-call(s32[1]{0:T(128)} %bitcast.6.refs_0_, bf16[832,512]{1,0:T(8,128)(2,1)S(1)} %bitcast.35, bf16[128,512]{1,0:T(8,128)(2,1)} %pad.4.refs_2_.refs_8_, f32[1,2048]{1,0:T(1,128)} %refs_3_.3, ...), custom_call_target="tpu_custom_call" | custom-call | flops 10000000 | bytes 1000 | tf_op jit(solution)/shard_map/forward/pallas_call | solution.py:176
  51.1 6.6 %produce.1 = (bf16[832,512]{1,0:T(8,128)(2,1)}, bf16[832,512]{1,0:T(8,128)(2,1)}) custom-call(bf16[832,2048]{1,0:T(8,128)(2,1)} %get-tuple-element.74.refs_0_.refs_3_, bf16[2048,512]{1,0:T(8,128)(2,1)} %bitcast.50, f32[1,512]{1,0:T(1,128)} %refs_2_.3, f32[832,128]{1,0:T(8,128)} %get-tuple-element.75.refs_3_.refs_2_), custom_call_target="tpu_custom_call" | custom-call | flops 10000000 | bytes 1000 | tf_op jit(solution)/shard_map/produce/pallas_call | solution.py:87
  57.7 4.7 %all-to-all-done.1 = bf16[8,104,512]{2,1,0:T(8,128)(2,1)S(1)} async-done(((bf16[8,104,512]{2,1,0:T(8,128)(2,1)}), bf16[8,104,512]{2,1,0:T(8,128)(2,1)S(1)}, u32[]{:S(2)}, u32[]{:S(2)}) %all-to-all-start.1) | async-done | bytes 852000 | tf_op jit(solution)/shard_map/all_to_all | solution.py:724
  62.4 9.1 %experts.1 = (bf16[832,2048]{1,0:T(8,128)(2,1)}, bf16[832,512]{1,0:T(8,128)(2,1)}, bf16[832,128]{1,0:T(8,128)(2,1)}) custom-call(s32[1]{0:T(128)} %bitcast.6.refs_0_, bf16[832,512]{1,0:T(8,128)(2,1)S(1)} %bitcast.29, f32[832,128]{1,0:T(8,128)} %get-tuple-element.75.refs_3_.refs_2_, bf16[2048,512]{1,0:T(8,128)(2,1)} %bitcast.51, ...), custom_call_target="tpu_custom_call" | custom-call | flops 10000000 | bytes 1000 | tf_op jit(solution)/shard_map/experts/pallas_call | solution.py:176
  71.6 4.5 %all-to-all-start.3 = ((bf16[8,104,512]{2,1,0:T(8,128)(2,1)}), bf16[8,104,512]{2,1,0:T(8,128)(2,1)S(1)}, u32[]{:S(2)}, u32[]{:S(2)}) async-start(bf16[8,104,512]{2,1,0:T(8,128)(2,1)} %bitcast.17), calls=%async_computation.3 | async-start | bytes 1703936 | tf_op jit(solution)/shard_map/all_to_all | solution.py:724
  78.6 8.4 %forward.3 = (bf16[832,2048]{1,0:T(8,128)(2,1)}, bf16[832,2048]{1,0:T(8,128)(2,1)}, f32[832,128]{1,0:T(8,128)}, f32[832,128]{1,0:T(8,128)}) custom-call(s32[1]{0:T(128)} %bitcast.6.refs_0_, bf16[832,512]{1,0:T(8,128)(2,1)} %copy-done, bf16[128,512]{1,0:T(8,128)(2,1)} %pad.4.refs_2_.refs_8_, f32[1,2048]{1,0:T(1,128)} %refs_3_.3, bf16[512,2048]{1,0:T(8,128)(2,1)} %bitcast.46, ...), custom_call_target="tpu_custom_call" | custom-call | flops 10000000 | bytes 1000 | tf_op jit(solution)/shard_map/forward/pallas_call | solution.py:176
  86.9 9.0 %expert_weights.2 = (bf16[4,1040,512]{2,1,0:T(8,128)(2,1)}, f32[8,512]{1,0:T(8,128)}) custom-call(bf16[832,512]{1,0:T(8,128)(2,1)S(1)} %bitcast.36, bf16[832,512]{1,0:T(8,128)(2,1)S(1)} %bitcast.31, f32[832,128]{1,0:T(8,128)} %get-tuple-element.75.refs_3_.refs_2_, bf16[832,2048]{1,0:T(8,128)(2,1)} %get-tuple-element.74.refs_0_.refs_3_, ...), custom_call_target="tpu_custom_call" | custom-call | flops 10000000 | bytes 1000 | tf_op jit(solution)/shard_map/expert_weights/pallas_call | solution.py:87
  97.0 4.9 %all-to-all-start.2 = ((bf16[8,104,512]{2,1,0:T(8,128)(2,1)}), bf16[8,104,512]{2,1,0:T(8,128)(2,1)S(1)}, u32[]{:S(2)}, u32[]{:S(2)}) async-start(bf16[8,104,512]{2,1,0:T(8,128)(2,1)} %bitcast.58), calls=%async_computation.2 | async-start | bytes 1703936 | tf_op jit(solution)/shard_map/all_to_all | solution.py:724
  101.9 9.7 %backward.1 = (bf16[1040,512]{1,0:T(8,128)(2,1)}, bf16[1040,512]{1,0:T(8,128)(2,1)}, bf16[384,512]{1,0:T(8,128)(2,1)}) custom-call(s32[1]{0:T(128)} %bitcast.16.refs_0_, bf16[832,512]{1,0:T(8,128)(2,1)S(1)} %bitcast.37, f32[384,8]{1,0:T(8,128)} %get-tuple-element.71.refs_0_.refs_2_, f32[384,512]{1,0:T(8,128)} %get-tuple-element.72.refs_1_.refs_3_, ...), custom_call_target="tpu_custom_call" | custom-call | flops 10000000 | bytes 1000 | tf_op jit(solution)/shard_map/backward/pallas_call | solution.py:176
  111.7 2.9 %collective-permute-done.2.refs_2_ = bf16[1040,512]{1,0:T(8,128)(2,1)S(1)} collective-permute-done((bf16[1040,512]{1,0:T(8,128)(2,1)}, bf16[1040,512]{1,0:T(8,128)(2,1)S(1)}, u32[]{:S(2)}, u32[]{:S(2)}) %collective-permute-start.2) | collective-permute-done | bytes 1064992 | tf_op jit(solution)/shard_map/ppermute | solution.py:677
  116.1 2.1 %collective-permute-start.3 = (bf16[272,512]{1,0:T(8,128)(2,1)S(1)}, bf16[272,512]{1,0:T(8,128)(2,1)S(1)}, u32[]{:S(2)}, u32[]{:S(2)}) collective-permute-start(bf16[272,512]{1,0:T(8,128)(2,1)S(1)} %get-tuple-element.97), channel_id=1, source_target_pairs={{0,1},{1,0},{2,3},{3,2},{4,5},{5,4},{6,7},{7,6},{8,9},{9,8},{10,11... | collective-permute-start | bytes 835592 | tf_op jit(solution)/shard_map/ppermute | solution.py:679
  119.7 11.7 %expert_weights.3.refs_5_.refs_0_ = bf16[4,1040,512]{2,1,0:T(8,128)(2,1)} custom-call(bf16[832,512]{1,0:T(8,128)(2,1)} %copy-done, bf16[832,512]{1,0:T(8,128)(2,1)} %copy-done.1, f32[832,128]{1,0:T(8,128)} %get-tuple-element.100.refs_2_, bf16[832,2048]{1,0:T(8,128)(2,1)} %get-tuple-element.101.refs_3_, bf16[832,2048]{1,0:T(8,128)(2,1)} %get-tuple-element.82.refs_6_.refs_4_, ...), custom_call_target="tpu_custom_call" | custom-call | flops 10000000 | bytes 1000 | tf_op jit(solution)/shard_map/expert_weights/pallas_call | solution.py:87
  134.3 2.4 %collective-permute-start.7 = (bf16[80,512]{1,0:T(8,128)(2,1)S(1)}, bf16[80,512]{1,0:T(8,128)(2,1)S(1)}, u32[]{:S(2)}, u32[]{:S(2)}) collective-permute-start(bf16[80,512]{1,0:T(8,128)(2,1)S(1)} %get-tuple-element.104), channel_id=1, source_target_pairs={{0,4},{1,5},{2,6},{3,7},{4,0},{5,1},{6,2},{7,3},{8,12},{9,13},{10,... | collective-permute-start | bytes 245768 | tf_op jit(solution)/shard_map/ppermute | solution.py:679
  137.0 2.6 %combine.1.refs_4_ = bf16[384,512]{1,0:T(8,128)(2,1)} custom-call(f32[384,8]{1,0:T(8,128)} %get-tuple-element.71.refs_0_.refs_2_, f32[384,512]{1,0:T(8,128)} %get-tuple-element.72.refs_1_.refs_3_, bf16[832,512]{1,0:T(8,128)(2,1)S(1)} %bitcast.33), custom_call_target="tpu_custom_call" | custom-call | flops 10000000 | bytes 1000 | tf_op jit(solution)/shard_map/combine/pallas_call | solution.py:87
  139.7 4.2 %collective-permute-done.7.refs_2_ = bf16[80,512]{1,0:T(8,128)(2,1)S(1)} collective-permute-done((bf16[80,512]{1,0:T(8,128)(2,1)S(1)}, bf16[80,512]{1,0:T(8,128)(2,1)S(1)}, u32[]{:S(2)}, u32[]{:S(2)}) %collective-permute-start.7) | collective-permute-done | bytes 81952 | tf_op jit(solution)/shard_map/ppermute | solution.py:679
  148.4 3.4 %finish_experts.2 = (f32[512,2048]{1,0:T(8,128)}, f32[1,2048]{1,0:T(1,128)}, f32[2048,512]{1,0:T(8,128)}, f32[1,512]{1,0:T(1,128)}) custom-call(bf16[4,1040,512]{2,1,0:T(8,128)(2,1)} %pass.4.refs_0_, bf16[4,1040,512]{2,1,0:T(8,128)(2,1)S(1)} %collective-permute-done.12.refs_1_, bf16[64,512]{1,0:T(8,128)(2,1)S(1)} %get-tuple-element.106.refs_2_.refs_0_), custom_call_target="tpu_custom_call" | custom-call | flops 10000000 | bytes 1000 | tf_op jit(solution)/shard_map/finish_experts/pallas_call | solution.py:87
  156.9 3.4 %finish_experts.3 = (f32[512,2048]{1,0:T(8,128)}, f32[1,2048]{1,0:T(1,128)}, f32[2048,512]{1,0:T(8,128)}, f32[1,512]{1,0:T(1,128)}) custom-call(bf16[4,1040,512]{2,1,0:T(8,128)(2,1)} %pass.4.refs_0_, bf16[4,1040,512]{2,1,0:T(8,128)(2,1)S(1)} %collective-permute-done.12.refs_1_, ...), custom_call_target="tpu_custom_call", output_to_operand_aliasing={{0}: (2, {}), {1}: (3, {}), {2}: (4, {}), {3}: (5, {})} | custom-call | flops 10000000 | bytes 1000 | tf_op jit(solution)/shard_map/finish_experts/pallas_call | solution.py:87
  163.6 2.8 %collective-permute-done.15.refs_0_ = bf16[256,512]{1,0:T(8,128)(2,1)S(1)} collective-permute-done((bf16[256,512]{1,0:T(8,128)(2,1)S(1)}, bf16[256,512]{1,0:T(8,128)(2,1)S(1)}, u32[]{:S(2)}, u32[]{:S(2)}) %collective-permute-start.15) | collective-permute-done | bytes 262176 | tf_op jit(solution)/shard_map/ppermute | solution.py:683
  167.9 3.0 %finish_shared.1 = (f32[512,512]{1,0:T(8,128)}, f32[512,512]{1,0:T(8,128)}, f32[512,512]{1,0:T(8,128)}, f32[512,512]{1,0:T(8,128)}, f32[1,512]{1,0:T(1,128)}, /*...) custom-call(s32[3]{0:T(128)S(1)} %pad_add_fusion.refs_0_, ...), custom_call_target="tpu_custom_call" | custom-call | flops 3000000000 | bytes 300000 | tf_op jit(solution)/shard_map/finish_shared/pallas_call | solution.py:87
  (53 shorter events, 26.6 us)
Async XLA Ops:
  8.1 28.9 %all-to-all-start = ((bf16[8,104,512]{2,1,0:T(8,128)(2,1)}), bf16[8,104,512]{2,1,0:T(8,128)(2,1)S(1)}, u32[]{:S(2)}, u32[]{:S(2)}) async-start(bf16[8,104,512]{2,1,0:T(8,128)(2,1)} %bitcast.7), calls=%async_computation | async-start | bytes 1703936 | tf_op jit(solution)/shard_map/all_to_all | solution.py:724
  37.1 25.3 %all-to-all-start.1 = ((bf16[8,104,512]{2,1,0:T(8,128)(2,1)}), bf16[8,104,512]{2,1,0:T(8,128)(2,1)S(1)}, u32[]{:S(2)}, u32[]{:S(2)}) async-start(bf16[8,104,512]{2,1,0:T(8,128)(2,1)} %bitcast.59), calls=%async_computation.1 | async-start | bytes 1703936 | tf_op jit(solution)/shard_map/all_to_all | solution.py:724
  40.8 21.6 %collective-permute-start = (bf16[832,512]{1,0:T(8,128)(2,1)S(1)}, bf16[832,512]{1,0:T(8,128)(2,1)S(1)}, u32[]{:S(2)}, u32[]{:S(2)}) collective-permute-start(bf16[832,512]{1,0:T(8,128)(2,1)S(1)} %bitcast.34), channel_id=1, source_target_pairs={{0,16},{8,24},{16,0},{24,8},{1,17},{9,25},{17,1},{25,9},{2,18},{10... | collective-permute-start | bytes 2555912 | tf_op jit(solution)/shard_map/ppermute | solution.py:677
  71.6 25.4 %all-to-all-start.3 = ((bf16[8,104,512]{2,1,0:T(8,128)(2,1)}), bf16[8,104,512]{2,1,0:T(8,128)(2,1)S(1)}, u32[]{:S(2)}, u32[]{:S(2)}) async-start(bf16[8,104,512]{2,1,0:T(8,128)(2,1)} %bitcast.17), calls=%async_computation.3 | async-start | bytes 1703936 | tf_op jit(solution)/shard_map/all_to_all | solution.py:724
  77.0 24.9 %collective-permute-start.1 = (bf16[832,512]{1,0:T(8,128)(2,1)}, bf16[832,512]{1,0:T(8,128)(2,1)S(1)}, u32[]{:S(2)}, u32[]{:S(2)}) collective-permute-start(bf16[832,512]{1,0:T(8,128)(2,1)} %copy_rows.1), channel_id=1, source_target_pairs={{0,16},{8,24},{16,0},{24,8},{1,17},{9,25},{17,1},{25,9},{2,18},{10... | collective-permute-start | bytes 2555912 | tf_op jit(solution)/shard_map/ppermute | solution.py:677
  97.0 34.4 %all-to-all-start.2 = ((bf16[8,104,512]{2,1,0:T(8,128)(2,1)}), bf16[8,104,512]{2,1,0:T(8,128)(2,1)S(1)}, u32[]{:S(2)}, u32[]{:S(2)}) async-start(bf16[8,104,512]{2,1,0:T(8,128)(2,1)} %bitcast.58), calls=%async_computation.2 | async-start | bytes 1703936 | tf_op jit(solution)/shard_map/all_to_all | solution.py:724
  111.7 3.0 %collective-permute-start.2 = (bf16[1040,512]{1,0:T(8,128)(2,1)}, bf16[1040,512]{1,0:T(8,128)(2,1)S(1)}, u32[]{:S(2)}, u32[]{:S(2)}) collective-permute-start(bf16[1040,512]{1,0:T(8,128)(2,1)} %get-tuple-element.95), channel_id=1, source_target_pairs={{0,8},{8,0},{16,24},{24,16},{1,9},{9,1},{17,25},{25,17},{2,10},{10... | collective-permute-start | bytes 3194888 | tf_op jit(solution)/shard_map/ppermute | solution.py:677
  116.1 15.3 %collective-permute-start.3 = (bf16[272,512]{1,0:T(8,128)(2,1)S(1)}, bf16[272,512]{1,0:T(8,128)(2,1)S(1)}, u32[]{:S(2)}, u32[]{:S(2)}) collective-permute-start(bf16[272,512]{1,0:T(8,128)(2,1)S(1)} %get-tuple-element.97), channel_id=1, source_target_pairs={{0,1},{1,0},{2,3},{3,2},{4,5},{5,4},{6,7},{7,6},{8,9},{9,8},{10,11... | collective-permute-start | bytes 835592 | tf_op jit(solution)/shard_map/ppermute | solution.py:679
  118.2 13.2 %collective-permute-start.4 = (bf16[272,512]{1,0:T(8,128)(2,1)S(1)}, bf16[272,512]{1,0:T(8,128)(2,1)S(1)}, u32[]{:S(2)}, u32[]{:S(2)}) collective-permute-start(bf16[272,512]{1,0:T(8,128)(2,1)S(1)} %get-tuple-element.98), channel_id=1, source_target_pairs={{0,16},{8,24},{16,0},{24,8},{1,17},{9,25},{17,1},{25,9},{2,18},{10... | collective-permute-start | bytes 835592 | tf_op jit(solution)/shard_map/ppermute | solution.py:677
  118.7 13.6 %collective-permute-start.5 = (bf16[272,512]{1,0:T(8,128)(2,1)S(1)}, bf16[272,512]{1,0:T(8,128)(2,1)S(1)}, u32[]{:S(2)}, u32[]{:S(2)}) collective-permute-start(bf16[272,512]{1,0:T(8,128)(2,1)S(1)} %get-tuple-element.99), channel_id=1, source_target_pairs={{0,17},{1,16},{2,19},{3,18},{4,21},{5,20},{6,23},{7,22},{8,25},{9,... | collective-permute-start | bytes 835592 | tf_op jit(solution)/shard_map/ppermute | solution.py:683
  132.5 15.9 %collective-permute-start.12 = (bf16[4,1040,512]{2,1,0:T(8,128)(2,1)}, bf16[4,1040,512]{2,1,0:T(8,128)(2,1)S(1)}, u32[]{:S(2)}, u32[]{:S(2)}) collective-permute-start(bf16[4,1040,512]{2,1,0:T(8,128)(2,1)} %pass.4.refs_0_), channel_id=1, source_target_pairs={{0,8},{8,0},{16,24},{24,16},{1,9},{9,1},{17,25},{25,17},{2,10},{10... | collective-permute-start | bytes 12779528 | tf_op jit(solution)/shard_map/ppermute | solution.py:677
  132.6 7.1 %collective-permute-start.6 = (bf16[80,512]{1,0:T(8,128)(2,1)S(1)}, bf16[80,512]{1,0:T(8,128)(2,1)S(1)}, u32[]{:S(2)}, u32[]{:S(2)}) collective-permute-start(bf16[80,512]{1,0:T(8,128)(2,1)S(1)} %get-tuple-element.103), channel_id=1, source_target_pairs={{0,2},{1,3},{2,0},{3,1},{4,6},{5,7},{6,4},{7,5},{8,10},{9,11},{10,... | collective-permute-start | bytes 245768 | tf_op jit(solution)/shard_map/ppermute | solution.py:679
  134.3 9.6 %collective-permute-start.7 = (bf16[80,512]{1,0:T(8,128)(2,1)S(1)}, bf16[80,512]{1,0:T(8,128)(2,1)S(1)}, u32[]{:S(2)}, u32[]{:S(2)}) collective-permute-start(bf16[80,512]{1,0:T(8,128)(2,1)S(1)} %get-tuple-element.104), channel_id=1, source_target_pairs={{0,4},{1,5},{2,6},{3,7},{4,0},{5,1},{6,2},{7,3},{8,12},{9,13},{10,... | collective-permute-start | bytes 245768 | tf_op jit(solution)/shard_map/ppermute | solution.py:679
  136.7 7.2 %collective-permute-start.8 = (bf16[80,512]{1,0:T(8,128)(2,1)S(1)}, bf16[80,512]{1,0:T(8,128)(2,1)S(1)}, u32[]{:S(2)}, u32[]{:S(2)}) collective-permute-start(bf16[80,512]{1,0:T(8,128)(2,1)S(1)} %get-tuple-element.105), channel_id=1, source_target_pairs={{0,6},{1,7},{2,4},{3,5},{4,2},{5,3},{6,0},{7,1},{8,14},{9,15},{10,... | collective-permute-start | bytes 245768 | tf_op jit(solution)/shard_map/ppermute | solution.py:679
  144.0 7.8 %collective-permute-start.9 = (bf16[64,512]{1,0:T(8,128)(2,1)S(1)}, bf16[64,512]{1,0:T(8,128)(2,1)S(1)}, u32[]{:S(2)}, u32[]{:S(2)}) collective-permute-start(bf16[64,512]{1,0:T(8,128)(2,1)S(1)} %get-tuple-element.106.refs_2_.refs_0_), channel_id=1, source_target_pairs={{0,2},{1,3},{2,0},{3,1},{4,6},{5,7},{6,4},{7,5},{8,10},{9,11},{10,... | collective-permute-start | bytes 196616 | tf_op jit(solution)/shard_map/ppermute | solution.py:679
  145.7 7.6 %collective-permute-start.10 = (bf16[64,512]{1,0:T(8,128)(2,1)S(1)}, bf16[64,512]{1,0:T(8,128)(2,1)S(1)}, u32[]{:S(2)}, u32[]{:S(2)}) collective-permute-start(bf16[64,512]{1,0:T(8,128)(2,1)S(1)} %get-tuple-element.106.refs_2_.refs_0_), channel_id=1, source_target_pairs={{0,4},{1,5},{2,6},{3,7},{4,0},{5,1},{6,2},{7,3},{8,12},{9,13},{10,... | collective-permute-start | bytes 196616 | tf_op jit(solution)/shard_map/ppermute | solution.py:679
  147.1 6.2 %collective-permute-start.11 = (bf16[64,512]{1,0:T(8,128)(2,1)S(1)}, bf16[64,512]{1,0:T(8,128)(2,1)S(1)}, u32[]{:S(2)}, u32[]{:S(2)}) collective-permute-start(bf16[64,512]{1,0:T(8,128)(2,1)S(1)} %get-tuple-element.106.refs_2_.refs_0_), channel_id=1, source_target_pairs={{0,6},{1,7},{2,4},{3,5},{4,2},{5,3},{6,0},{7,1},{8,14},{9,15},{10,... | collective-permute-start | bytes 196616 | tf_op jit(solution)/shard_map/ppermute | solution.py:679
  153.3 8.7 %collective-permute-start.13 = (bf16[256,512]{1,0:T(8,128)(2,1)S(1)}, bf16[256,512]{1,0:T(8,128)(2,1)S(1)}, u32[]{:S(2)}, u32[]{:S(2)}) collective-permute-start(bf16[256,512]{1,0:T(8,128)(2,1)S(1)} %gather.1.refs_6_.refs_1_), channel_id=1, source_target_pairs={{0,1},{1,0},{2,3},{3,2},{4,5},{5,4},{6,7},{7,6},{8,9},{9,8},{10,11... | collective-permute-start | bytes 786440 | tf_op jit(solution)/shard_map/ppermute | solution.py:679
  154.8 8.7 %collective-permute-start.14 = (bf16[256,512]{1,0:T(8,128)(2,1)S(1)}, bf16[256,512]{1,0:T(8,128)(2,1)S(1)}, u32[]{:S(2)}, u32[]{:S(2)}) collective-permute-start(bf16[256,512]{1,0:T(8,128)(2,1)S(1)} %gather.1.refs_6_.refs_1_), channel_id=1, source_target_pairs={{0,16},{8,24},{16,0},{24,8},{1,17},{9,25},{17,1},{25,9},{2,18},{10... | collective-permute-start | bytes 786440 | tf_op jit(solution)/shard_map/ppermute | solution.py:677
  155.4 11.0 %collective-permute-start.15 = (bf16[256,512]{1,0:T(8,128)(2,1)S(1)}, bf16[256,512]{1,0:T(8,128)(2,1)S(1)}, u32[]{:S(2)}, u32[]{:S(2)}) collective-permute-start(bf16[256,512]{1,0:T(8,128)(2,1)S(1)} %gather.1.refs_6_.refs_1_), channel_id=1, source_target_pairs={{0,17},{1,16},{2,19},{3,18},{4,21},{5,20},{6,23},{7,22},{8,25},{9,... | collective-permute-start | bytes 786440 | tf_op jit(solution)/shard_map/ppermute | solution.py:683
  156.9 9.6 %collective-permute-start.16 = (bf16[256,512]{1,0:T(8,128)(2,1)S(1)}, bf16[256,512]{1,0:T(8,128)(2,1)S(1)}, u32[]{:S(2)}, u32[]{:S(2)}) collective-permute-start(bf16[256,512]{1,0:T(8,128)(2,1)S(1)} %gather.1.refs_6_.refs_1_), channel_id=1, source_target_pairs={{0,8},{8,0},{16,24},{24,16},{1,9},{9,1},{17,25},{25,17},{2,10},{10... | collective-permute-start | bytes 786440 | tf_op jit(solution)/shard_map/ppermute | solution.py:677
  162.0 4.4 %collective-permute-start.17 = (bf16[256,512]{1,0:T(8,128)(2,1)S(1)}, bf16[256,512]{1,0:T(8,128)(2,1)S(1)}, u32[]{:S(2)}, u32[]{:S(2)}) collective-permute-start(bf16[256,512]{1,0:T(8,128)(2,1)S(1)} %collective-permute-done.13.refs_2_), channel_id=1, source_target_pairs={{0,8},{8,0},{16,24},{24,16},{1,9},{9,1},{17,25},{25,17},{2,10},{10... | collective-permute-start | bytes 786440 | tf_op jit(solution)/shard_map/ppermute | solution.py:677
  163.6 2.9 %collective-permute-start.18 = (bf16[256,512]{1,0:T(8,128)(2,1)S(1)}, bf16[256,512]{1,0:T(8,128)(2,1)S(1)}, u32[]{:S(2)}, u32[]{:S(2)}) collective-permute-start(bf16[256,512]{1,0:T(8,128)(2,1)S(1)} %collective-permute-done.14.refs_3_), channel_id=1, source_target_pairs={{0,8},{8,0},{16,24},{24,16},{1,9},{9,1},{17,25},{25,17},{2,10},{10... | collective-permute-start | bytes 786440 | tf_op jit(solution)/shard_map/ppermute | solution.py:677
  166.4 1.5 collective-permute-start.19
  (3 other events, 53.1 us)

commit v3 on v2

--- a/solution.py
+++ b/solution.py
@@ -385,16 +385,19 @@
             ref[...] = (produced[:, at * size : (at + 1) * size].astype(F32) * gate).astype(BF16)
 
 
-def expert_kernel(experts, tile, me_ref, grad_ref, gate_ref, *refs):
-    steps = (len(refs) - 6) // 3
-    downs, slopes, ups = [refs[0], *refs[6 : 3 * steps + 3 : 3]], [refs[1], *refs[7 : 3 * steps + 3 : 3]], [refs[2], *refs[8 : 3 * steps + 3 : 3]]
-    produced_ref, gates_ref, router_ref = refs[3:6]
-    inner_grad_ref, rows_grad_ref, logit_grad_ref = refs[3 * steps + 3 :]
+def expert_kernel(experts, tile, me_ref, grad_ref, *refs):
+    steps = (len(refs) - 7) // 3
+    gate_ref, produced_ref, gates_ref, router_ref = refs[1], *refs[3:6]
+    pairs = [(refs[0], refs[2])] + [refs[at : at + 2] for at in range(6, 2 * steps + 4, 2)]
+    downs, slopes = zip(*pairs)
+    ups = refs[2 * steps + 4 : 3 * steps + 4]
+    inner_grad_ref, rows_grad_ref, logit_grad_ref = refs[3 * steps + 4 :]
     total, width = grad_ref.shape
-    gate = jnp.concatenate([gate_ref[...]] * (tile // LANES), axis=1)
     for step in range(steps):
         lanes = slice(step * tile, (step + 1) * tile)
-        made = dot_nt(grad_ref[...], downs[step][...]) * gate * slopes[step][...].astype(F32)
+        made = dot_nt(grad_ref[...], downs[step][...])
+        gate = jnp.concatenate([gate_ref[...]] * (tile // LANES), axis=1)
+        made = made * gate * slopes[step][...].astype(F32)
         inner_grad_ref[:, lanes] = made.astype(BF16)
         inner_grad_ref.flush(slice(None), lanes)
         if step == 0:
@@ -786,13 +789,15 @@
         )
         grad_rows = Held(grad_rows)
 
-        def triple(at):
-            return Part(down_w, tile, at, rows=True), Part(slope, tile, at), Part(up_w, tile, at)
-
+        def pair_of(at):
+            return Part(down_w, tile, at, rows=True), Part(slope, tile, at)
+
+        down_first, slope_first = pair_of(0)
+        later = [part for at in range(1, steps) for part in pair_of(at)] + [Part(up_w, tile, at) for at in range(steps)]
         rows_others = [hop(rows.value, bits, 0) for bits in range(2, narrow, 2)]
         inner_grad, rows_grad, logit_grad = fuse(
             functools.partial(expert_kernel, experts, tile),
-            (me, grad_rows, gate, *triple(0), produced, gates, router_t, *(part for at in range(1, steps) for part in triple(at))),
+            (me, grad_rows, down_first, gate, slope_first, produced, gates, router_t, *later),
             (far((slots_all, hidden_width), BF16), held((slots_all, width), BF16), far((slots_all, LANES), BF16)),
             40,
             0.01,

time: 172 us -> 172 us (level)
  no operation moved by 1% of the time
where the time goes in v3:
time: 172 us; the launch traced here: 171 us
  Pallas kernels  87.8 us (51%)
  waiting for transfers between devices  41.7 us (24%)
  starting transfers between devices  39.8 us (23%)
    pallas_call x16, Pallas kernels, run(): pl.pallas_call(body, grid=grid, in_specs=list(in_specs) + [loose(value) f...  45.1 us
    pallas_call x5, Pallas kernels, fuse(): pl.pallas_call(body, in_specs=[spec(a) for a in args] + [loose(value) for...  42.7 us
    all_to_all x4, waiting for transfers between devices, exchange(): lax.all_to_all(value, 'wide', split_axis=0, concat_axis=0, tiled=True)  24.7 us
    all_to_all x4, starting transfers between devices, exchange(): lax.all_to_all(value, 'wide', split_axis=0, concat_axis=0, tiled=True)  20.5 us
    ppermute x8, starting transfers between devices, hop(): lax.ppermute(value, 'wide', [(i, i ^ wide_bits) for i in range(wide)])  12.5 us
    ppermute x8, waiting for transfers between devices, hop(): lax.ppermute(value, 'wide', [(i, i ^ wide_bits) for i in range(wide)])  7.47 us
    ppermute x10, waiting for transfers between devices, hop(): lax.ppermute(value, 'narrow', [(i, i ^ narrow_bits) for i in range(narrow)])  5.87 us
    ppermute x10, starting transfers between devices, hop(): lax.ppermute(value, 'narrow', [(i, i ^ narrow_bits) for i in range(narrow)])  4.34 us
  transfers between devices with their start and end apart: 24, of which 11 were waited for; matrix products, arithmetic and copies ran while one was open for 0% of the time, Pallas kernels for 40%

profile of v3, /device:TPU:0, one launch (start us, length us, event | category | flops | bytes accessed | tf_op | source)
XLA Modules:
  0.0 170.9 jit_solution(12841817685513533579)
XLA Ops:
  0.6 7.5 %attention.1 = (f32[384,8]{1,0:T(8,128)}, f32[8,128]{1,0:T(8,128)}, f32[384,512]{1,0:T(8,128)}, bf16[384,512]{1,0:T(8,128)(2,1)}, bf16[384,512]{1,0:T(8,128)(2,1...) custom-call(s32[2,384]{1,0:T(2,128)} %bitcast.65, ...), custom_call_target="tpu_custom_call" | custom-call | flops 10000000000 | bytes 1000000 | tf_op jit(solution)/shard_map/attention/pallas_call | solution.py:176
  8.1 7.3 %all-to-all-start = ((bf16[8,104,512]{2,1,0:T(8,128)(2,1)}), bf16[8,104,512]{2,1,0:T(8,128)(2,1)S(1)}, u32[]{:S(2)}, u32[]{:S(2)}) async-start(bf16[8,104,512]{2,1,0:T(8,128)(2,1)} %bitcast.7), calls=%async_computation | async-start | bytes 1703936 | tf_op jit(solution)/shard_map/all_to_all | solution.py:727
  15.4 2.8 %dispatch.1 = bf16[832,512]{1,0:T(8,128)(2,1)} custom-call(f32[384,8]{1,0:T(8,128)} %get-tuple-element.71.refs_0_.refs_2_, bf16[384,512]{1,0:T(8,128)(2,1)} %refs_5_.3, bf16[832,512]{1,0:T(8,128)(2,1)} %get-tuple-element.73.refs_2_), custom_call_target="tpu_custom_call" | custom-call | flops 1000000000 | bytes 100000 | tf_op jit(solution)/shard_map/dispatch/pallas_call | solution.py:87
  18.2 18.8 %all-to-all-done = bf16[8,104,512]{2,1,0:T(8,128)(2,1)S(1)} async-done(((bf16[8,104,512]{2,1,0:T(8,128)(2,1)}), bf16[8,104,512]{2,1,0:T(8,128)(2,1)S(1)}, u32[]{:S(2)}, u32[]{:S(2)}) %all-to-all-start) | async-done | bytes 852000 | tf_op jit(solution)/shard_map/all_to_all | solution.py:727
  37.1 3.7 %all-to-all-start.1 = ((bf16[8,104,512]{2,1,0:T(8,128)(2,1)}), bf16[8,104,512]{2,1,0:T(8,128)(2,1)S(1)}, u32[]{:S(2)}, u32[]{:S(2)}) async-start(bf16[8,104,512]{2,1,0:T(8,128)(2,1)} %bitcast.59), calls=%async_computation.1 | async-start | bytes 1703936 | tf_op jit(solution)/shard_map/all_to_all | solution.py:727
  43.0 8.1 %forward.2 = (bf16[832,2048]{1,0:T(8,128)(2,1)}, bf16[832,2048]{1,0:T(8,128)(2,1)}, f32[832,128]{1,0:T(8,128)}, f32[832,128]{1,0:T(8,128)}) custom-call(s32[1]{0:T(128)} %bitcast.6.refs_0_, bf16[832,512]{1,0:T(8,128)(2,1)S(1)} %bitcast.35, bf16[128,512]{1,0:T(8,128)(2,1)} %pad.4.refs_2_.refs_7_, f32[1,2048]{1,0:T(1,128)} %refs_3_.3, ...), custom_call_target="tpu_custom_call" | custom-call | flops 10000000 | bytes 1000 | tf_op jit(solution)/shard_map/forward/pallas_call | solution.py:176
  51.1 6.6 %produce.1 = (bf16[832,512]{1,0:T(8,128)(2,1)}, bf16[832,512]{1,0:T(8,128)(2,1)}) custom-call(bf16[832,2048]{1,0:T(8,128)(2,1)} %get-tuple-element.74.refs_0_.refs_3_, bf16[2048,512]{1,0:T(8,128)(2,1)} %bitcast.50, f32[1,512]{1,0:T(1,128)} %refs_2_.3, f32[832,128]{1,0:T(8,128)} %get-tuple-element.75.refs_3_.refs_2_), custom_call_target="tpu_custom_call" | custom-call | flops 10000000 | bytes 1000 | tf_op jit(solution)/shard_map/produce/pallas_call | solution.py:87
  57.7 4.7 %all-to-all-done.1 = bf16[8,104,512]{2,1,0:T(8,128)(2,1)S(1)} async-done(((bf16[8,104,512]{2,1,0:T(8,128)(2,1)}), bf16[8,104,512]{2,1,0:T(8,128)(2,1)S(1)}, u32[]{:S(2)}, u32[]{:S(2)}) %all-to-all-start.1) | async-done | bytes 852000 | tf_op jit(solution)/shard_map/all_to_all | solution.py:727
  62.4 9.1 %experts.1 = (bf16[832,2048]{1,0:T(8,128)(2,1)}, bf16[832,512]{1,0:T(8,128)(2,1)}, bf16[832,128]{1,0:T(8,128)(2,1)}) custom-call(s32[1]{0:T(128)} %bitcast.6.refs_0_, bf16[832,512]{1,0:T(8,128)(2,1)S(1)} %bitcast.29, bf16[2048,512]{1,0:T(8,128)(2,1)} %bitcast.51, f32[832,128]{1,0:T(8,128)} %get-tuple-element.75.refs_3_.refs_2_, ...), custom_call_target="tpu_custom_call" | custom-call | flops 10000000 | bytes 1000 | tf_op jit(solution)/shard_map/experts/pallas_call | solution.py:176
  71.5 4.5 %all-to-all-start.3 = ((bf16[8,104,512]{2,1,0:T(8,128)(2,1)}), bf16[8,104,512]{2,1,0:T(8,128)(2,1)S(1)}, u32[]{:S(2)}, u32[]{:S(2)}) async-start(bf16[8,104,512]{2,1,0:T(8,128)(2,1)} %bitcast.17), calls=%async_computation.3 | async-start | bytes 1703936 | tf_op jit(solution)/shard_map/all_to_all | solution.py:727
  78.6 8.4 %forward.3 = (bf16[832,2048]{1,0:T(8,128)(2,1)}, bf16[832,2048]{1,0:T(8,128)(2,1)}, f32[832,128]{1,0:T(8,128)}, f32[832,128]{1,0:T(8,128)}) custom-call(s32[1]{0:T(128)} %bitcast.6.refs_0_, bf16[832,512]{1,0:T(8,128)(2,1)} %copy-done, bf16[128,512]{1,0:T(8,128)(2,1)} %pad.4.refs_2_.refs_7_, f32[1,2048]{1,0:T(1,128)} %refs_3_.3, bf16[512,2048]{1,0:T(8,128)(2,1)} %bitcast.46, ...), custom_call_target="tpu_custom_call" | custom-call | flops 10000000 | bytes 1000 | tf_op jit(solution)/shard_map/forward/pallas_call | solution.py:176
  86.9 9.0 %expert_weights.2 = (bf16[4,1040,512]{2,1,0:T(8,128)(2,1)}, f32[8,512]{1,0:T(8,128)}) custom-call(bf16[832,512]{1,0:T(8,128)(2,1)S(1)} %bitcast.36, bf16[832,512]{1,0:T(8,128)(2,1)S(1)} %bitcast.31, f32[832,128]{1,0:T(8,128)} %get-tuple-element.75.refs_3_.refs_2_, bf16[832,2048]{1,0:T(8,128)(2,1)} %get-tuple-element.74.refs_0_.refs_3_, ...), custom_call_target="tpu_custom_call" | custom-call | flops 10000000 | bytes 1000 | tf_op jit(solution)/shard_map/expert_weights/pallas_call | solution.py:87
  97.0 4.9 %all-to-all-start.2 = ((bf16[8,104,512]{2,1,0:T(8,128)(2,1)}), bf16[8,104,512]{2,1,0:T(8,128)(2,1)S(1)}, u32[]{:S(2)}, u32[]{:S(2)}) async-start(bf16[8,104,512]{2,1,0:T(8,128)(2,1)} %bitcast.58), calls=%async_computation.2 | async-start | bytes 1703936 | tf_op jit(solution)/shard_map/all_to_all | solution.py:727
  101.9 9.7 %backward.1 = (bf16[1040,512]{1,0:T(8,128)(2,1)}, bf16[1040,512]{1,0:T(8,128)(2,1)}, bf16[384,512]{1,0:T(8,128)(2,1)}) custom-call(s32[1]{0:T(128)} %bitcast.16.refs_0_, bf16[832,512]{1,0:T(8,128)(2,1)S(1)} %bitcast.37, f32[384,8]{1,0:T(8,128)} %get-tuple-element.71.refs_0_.refs_2_, f32[384,512]{1,0:T(8,128)} %get-tuple-element.72.refs_1_.refs_3_, ...), custom_call_target="tpu_custom_call" | custom-call | flops 10000000 | bytes 1000 | tf_op jit(solution)/shard_map/backward/pallas_call | solution.py:176
  111.7 2.9 %collective-permute-done.2.refs_2_ = bf16[1040,512]{1,0:T(8,128)(2,1)S(1)} collective-permute-done((bf16[1040,512]{1,0:T(8,128)(2,1)}, bf16[1040,512]{1,0:T(8,128)(2,1)S(1)}, u32[]{:S(2)}, u32[]{:S(2)}) %collective-permute-start.2) | collective-permute-done | bytes 1064992 | tf_op jit(solution)/shard_map/ppermute | solution.py:680
  116.1 2.1 %collective-permute-start.3 = (bf16[272,512]{1,0:T(8,128)(2,1)S(1)}, bf16[272,512]{1,0:T(8,128)(2,1)S(1)}, u32[]{:S(2)}, u32[]{:S(2)}) collective-permute-start(bf16[272,512]{1,0:T(8,128)(2,1)S(1)} %get-tuple-element.97), channel_id=1, source_target_pairs={{0,1},{1,0},{2,3},{3,2},{4,5},{5,4},{6,7},{7,6},{8,9},{9,8},{10,11... | collective-permute-start | bytes 835592 | tf_op jit(solution)/shard_map/ppermute | solution.py:682
  119.7 11.7 %expert_weights.3.refs_5_.refs_0_ = bf16[4,1040,512]{2,1,0:T(8,128)(2,1)} custom-call(bf16[832,512]{1,0:T(8,128)(2,1)} %copy-done, bf16[832,512]{1,0:T(8,128)(2,1)} %copy-done.1, f32[832,128]{1,0:T(8,128)} %get-tuple-element.100.refs_2_, bf16[832,2048]{1,0:T(8,128)(2,1)} %get-tuple-element.101.refs_3_, bf16[832,2048]{1,0:T(8,128)(2,1)} %get-tuple-element.82.refs_6_.refs_4_, ...), custom_call_target="tpu_custom_call" | custom-call | flops 10000000 | bytes 1000 | tf_op jit(solution)/shard_map/expert_weights/pallas_call | solution.py:87
  134.3 2.4 %collective-permute-start.7 = (bf16[80,512]{1,0:T(8,128)(2,1)S(1)}, bf16[80,512]{1,0:T(8,128)(2,1)S(1)}, u32[]{:S(2)}, u32[]{:S(2)}) collective-permute-start(bf16[80,512]{1,0:T(8,128)(2,1)S(1)} %get-tuple-element.104), channel_id=1, source_target_pairs={{0,4},{1,5},{2,6},{3,7},{4,0},{5,1},{6,2},{7,3},{8,12},{9,13},{10,... | collective-permute-start | bytes 245768 | tf_op jit(solution)/shard_map/ppermute | solution.py:682
  137.0 2.6 %combine.1.refs_4_ = bf16[384,512]{1,0:T(8,128)(2,1)} custom-call(f32[384,8]{1,0:T(8,128)} %get-tuple-element.71.refs_0_.refs_2_, f32[384,512]{1,0:T(8,128)} %get-tuple-element.72.refs_1_.refs_3_, bf16[832,512]{1,0:T(8,128)(2,1)S(1)} %bitcast.33), custom_call_target="tpu_custom_call" | custom-call | flops 10000000 | bytes 1000 | tf_op jit(solution)/shard_map/combine/pallas_call | solution.py:87
  139.7 4.2 %collective-permute-done.7.refs_2_ = bf16[80,512]{1,0:T(8,128)(2,1)S(1)} collective-permute-done((bf16[80,512]{1,0:T(8,128)(2,1)S(1)}, bf16[80,512]{1,0:T(8,128)(2,1)S(1)}, u32[]{:S(2)}, u32[]{:S(2)}) %collective-permute-start.7) | collective-permute-done | bytes 81952 | tf_op jit(solution)/shard_map/ppermute | solution.py:682
  148.4 3.4 %finish_experts.2 = (f32[512,2048]{1,0:T(8,128)}, f32[1,2048]{1,0:T(1,128)}, f32[2048,512]{1,0:T(8,128)}, f32[1,512]{1,0:T(1,128)}) custom-call(bf16[4,1040,512]{2,1,0:T(8,128)(2,1)} %pass.4.refs_0_, bf16[4,1040,512]{2,1,0:T(8,128)(2,1)S(1)} %collective-permute-done.12.refs_1_, bf16[64,512]{1,0:T(8,128)(2,1)S(1)} %get-tuple-element.106.refs_2_.refs_0_), custom_call_target="tpu_custom_call" | custom-call | flops 10000000 | bytes 1000 | tf_op jit(solution)/shard_map/finish_experts/pallas_call | solution.py:87
  156.9 3.4 %finish_experts.3 = (f32[512,2048]{1,0:T(8,128)}, f32[1,2048]{1,0:T(1,128)}, f32[2048,512]{1,0:T(8,128)}, f32[1,512]{1,0:T(1,128)}) custom-call(bf16[4,1040,512]{2,1,0:T(8,128)(2,1)} %pass.4.refs_0_, bf16[4,1040,512]{2,1,0:T(8,128)(2,1)S(1)} %collective-permute-done.12.refs_1_, ...), custom_call_target="tpu_custom_call", output_to_operand_aliasing={{0}: (2, {}), {1}: (3, {}), {2}: (4, {}), {3}: (5, {})} | custom-call | flops 10000000 | bytes 1000 | tf_op jit(solution)/shard_map/finish_experts/pallas_call | solution.py:87
  163.6 2.8 %collective-permute-done.15.refs_0_ = bf16[256,512]{1,0:T(8,128)(2,1)S(1)} collective-permute-done((bf16[256,512]{1,0:T(8,128)(2,1)S(1)}, bf16[256,512]{1,0:T(8,128)(2,1)S(1)}, u32[]{:S(2)}, u32[]{:S(2)}) %collective-permute-start.15) | collective-permute-done | bytes 262176 | tf_op jit(solution)/shard_map/ppermute | solution.py:686
  167.9 3.0 %finish_shared.1 = (f32[512,512]{1,0:T(8,128)}, f32[512,512]{1,0:T(8,128)}, f32[512,512]{1,0:T(8,128)}, f32[512,512]{1,0:T(8,128)}, f32[1,512]{1,0:T(1,128)}, /*...) custom-call(s32[3]{0:T(128)S(1)} %pad_add_fusion.refs_0_, ...), custom_call_target="tpu_custom_call" | custom-call | flops 3000000000 | bytes 300000 | tf_op jit(solution)/shard_map/finish_shared/pallas_call | solution.py:87
  (53 shorter events, 26.6 us)
Async XLA Ops:
  8.1 28.9 %all-to-all-start = ((bf16[8,104,512]{2,1,0:T(8,128)(2,1)}), bf16[8,104,512]{2,1,0:T(8,128)(2,1)S(1)}, u32[]{:S(2)}, u32[]{:S(2)}) async-start(bf16[8,104,512]{2,1,0:T(8,128)(2,1)} %bitcast.7), calls=%async_computation | async-start | bytes 1703936 | tf_op jit(solution)/shard_map/all_to_all | solution.py:727
  37.1 25.3 %all-to-all-start.1 = ((bf16[8,104,512]{2,1,0:T(8,128)(2,1)}), bf16[8,104,512]{2,1,0:T(8,128)(2,1)S(1)}, u32[]{:S(2)}, u32[]{:S(2)}) async-start(bf16[8,104,512]{2,1,0:T(8,128)(2,1)} %bitcast.59), calls=%async_computation.1 | async-start | bytes 1703936 | tf_op jit(solution)/shard_map/all_to_all | solution.py:727
  40.8 21.6 %collective-permute-start = (bf16[832,512]{1,0:T(8,128)(2,1)S(1)}, bf16[832,512]{1,0:T(8,128)(2,1)S(1)}, u32[]{:S(2)}, u32[]{:S(2)}) collective-permute-start(bf16[832,512]{1,0:T(8,128)(2,1)S(1)} %bitcast.34), channel_id=1, source_target_pairs={{0,16},{8,24},{16,0},{24,8},{1,17},{9,25},{17,1},{25,9},{2,18},{10... | collective-permute-start | bytes 2555912 | tf_op jit(solution)/shard_map/ppermute | solution.py:680
  71.5 25.4 %all-to-all-start.3 = ((bf16[8,104,512]{2,1,0:T(8,128)(2,1)}), bf16[8,104,512]{2,1,0:T(8,128)(2,1)S(1)}, u32[]{:S(2)}, u32[]{:S(2)}) async-start(bf16[8,104,512]{2,1,0:T(8,128)(2,1)} %bitcast.17), calls=%async_computation.3 | async-start | bytes 1703936 | tf_op jit(solution)/shard_map/all_to_all | solution.py:727
  77.0 24.9 %collective-permute-start.1 = (bf16[832,512]{1,0:T(8,128)(2,1)}, bf16[832,512]{1,0:T(8,128)(2,1)S(1)}, u32[]{:S(2)}, u32[]{:S(2)}) collective-permute-start(bf16[832,512]{1,0:T(8,128)(2,1)} %copy_rows.1), channel_id=1, source_target_pairs={{0,16},{8,24},{16,0},{24,8},{1,17},{9,25},{17,1},{25,9},{2,18},{10... | collective-permute-start | bytes 2555912 | tf_op jit(solution)/shard_map/ppermute | solution.py:680
  97.0 34.4 %all-to-all-start.2 = ((bf16[8,104,512]{2,1,0:T(8,128)(2,1)}), bf16[8,104,512]{2,1,0:T(8,128)(2,1)S(1)}, u32[]{:S(2)}, u32[]{:S(2)}) async-start(bf16[8,104,512]{2,1,0:T(8,128)(2,1)} %bitcast.58), calls=%async_computation.2 | async-start | bytes 1703936 | tf_op jit(solution)/shard_map/all_to_all | solution.py:727
  111.6 3.0 %collective-permute-start.2 = (bf16[1040,512]{1,0:T(8,128)(2,1)}, bf16[1040,512]{1,0:T(8,128)(2,1)S(1)}, u32[]{:S(2)}, u32[]{:S(2)}) collective-permute-start(bf16[1040,512]{1,0:T(8,128)(2,1)} %get-tuple-element.95), channel_id=1, source_target_pairs={{0,8},{8,0},{16,24},{24,16},{1,9},{9,1},{17,25},{25,17},{2,10},{10... | collective-permute-start | bytes 3194888 | tf_op jit(solution)/shard_map/ppermute | solution.py:680
  116.1 15.3 %collective-permute-start.3 = (bf16[272,512]{1,0:T(8,128)(2,1)S(1)}, bf16[272,512]{1,0:T(8,128)(2,1)S(1)}, u32[]{:S(2)}, u32[]{:S(2)}) collective-permute-start(bf16[272,512]{1,0:T(8,128)(2,1)S(1)} %get-tuple-element.97), channel_id=1, source_target_pairs={{0,1},{1,0},{2,3},{3,2},{4,5},{5,4},{6,7},{7,6},{8,9},{9,8},{10,11... | collective-permute-start | bytes 835592 | tf_op jit(solution)/shard_map/ppermute | solution.py:682
  118.2 13.2 %collective-permute-start.4 = (bf16[272,512]{1,0:T(8,128)(2,1)S(1)}, bf16[272,512]{1,0:T(8,128)(2,1)S(1)}, u32[]{:S(2)}, u32[]{:S(2)}) collective-permute-start(bf16[272,512]{1,0:T(8,128)(2,1)S(1)} %get-tuple-element.98), channel_id=1, source_target_pairs={{0,16},{8,24},{16,0},{24,8},{1,17},{9,25},{17,1},{25,9},{2,18},{10... | collective-permute-start | bytes 835592 | tf_op jit(solution)/shard_map/ppermute | solution.py:680
  118.7 13.6 %collective-permute-start.5 = (bf16[272,512]{1,0:T(8,128)(2,1)S(1)}, bf16[272,512]{1,0:T(8,128)(2,1)S(1)}, u32[]{:S(2)}, u32[]{:S(2)}) collective-permute-start(bf16[272,512]{1,0:T(8,128)(2,1)S(1)} %get-tuple-element.99), channel_id=1, source_target_pairs={{0,17},{1,16},{2,19},{3,18},{4,21},{5,20},{6,23},{7,22},{8,25},{9,... | collective-permute-start | bytes 835592 | tf_op jit(solution)/shard_map/ppermute | solution.py:686
  132.5 15.9 %collective-permute-start.12 = (bf16[4,1040,512]{2,1,0:T(8,128)(2,1)}, bf16[4,1040,512]{2,1,0:T(8,128)(2,1)S(1)}, u32[]{:S(2)}, u32[]{:S(2)}) collective-permute-start(bf16[4,1040,512]{2,1,0:T(8,128)(2,1)} %pass.4.refs_0_), channel_id=1, source_target_pairs={{0,8},{8,0},{16,24},{24,16},{1,9},{9,1},{17,25},{25,17},{2,10},{10... | collective-permute-start | bytes 12779528 | tf_op jit(solution)/shard_map/ppermute | solution.py:680
  132.6 7.1 %collective-permute-start.6 = (bf16[80,512]{1,0:T(8,128)(2,1)S(1)}, bf16[80,512]{1,0:T(8,128)(2,1)S(1)}, u32[]{:S(2)}, u32[]{:S(2)}) collective-permute-start(bf16[80,512]{1,0:T(8,128)(2,1)S(1)} %get-tuple-element.103), channel_id=1, source_target_pairs={{0,2},{1,3},{2,0},{3,1},{4,6},{5,7},{6,4},{7,5},{8,10},{9,11},{10,... | collective-permute-start | bytes 245768 | tf_op jit(solution)/shard_map/ppermute | solution.py:682
  134.3 9.6 %collective-permute-start.7 = (bf16[80,512]{1,0:T(8,128)(2,1)S(1)}, bf16[80,512]{1,0:T(8,128)(2,1)S(1)}, u32[]{:S(2)}, u32[]{:S(2)}) collective-permute-start(bf16[80,512]{1,0:T(8,128)(2,1)S(1)} %get-tuple-element.104), channel_id=1, source_target_pairs={{0,4},{1,5},{2,6},{3,7},{4,0},{5,1},{6,2},{7,3},{8,12},{9,13},{10,... | collective-permute-start | bytes 245768 | tf_op jit(solution)/shard_map/ppermute | solution.py:682
  136.7 7.2 %collective-permute-start.8 = (bf16[80,512]{1,0:T(8,128)(2,1)S(1)}, bf16[80,512]{1,0:T(8,128)(2,1)S(1)}, u32[]{:S(2)}, u32[]{:S(2)}) collective-permute-start(bf16[80,512]{1,0:T(8,128)(2,1)S(1)} %get-tuple-element.105), channel_id=1, source_target_pairs={{0,6},{1,7},{2,4},{3,5},{4,2},{5,3},{6,0},{7,1},{8,14},{9,15},{10,... | collective-permute-start | bytes 245768 | tf_op jit(solution)/shard_map/ppermute | solution.py:682
  143.9 7.8 %collective-permute-start.9 = (bf16[64,512]{1,0:T(8,128)(2,1)S(1)}, bf16[64,512]{1,0:T(8,128)(2,1)S(1)}, u32[]{:S(2)}, u32[]{:S(2)}) collective-permute-start(bf16[64,512]{1,0:T(8,128)(2,1)S(1)} %get-tuple-element.106.refs_2_.refs_0_), channel_id=1, source_target_pairs={{0,2},{1,3},{2,0},{3,1},{4,6},{5,7},{6,4},{7,5},{8,10},{9,11},{10,... | collective-permute-start | bytes 196616 | tf_op jit(solution)/shard_map/ppermute | solution.py:682
  145.7 7.6 %collective-permute-start.10 = (bf16[64,512]{1,0:T(8,128)(2,1)S(1)}, bf16[64,512]{1,0:T(8,128)(2,1)S(1)}, u32[]{:S(2)}, u32[]{:S(2)}) collective-permute-start(bf16[64,512]{1,0:T(8,128)(2,1)S(1)} %get-tuple-element.106.refs_2_.refs_0_), channel_id=1, source_target_pairs={{0,4},{1,5},{2,6},{3,7},{4,0},{5,1},{6,2},{7,3},{8,12},{9,13},{10,... | collective-permute-start | bytes 196616 | tf_op jit(solution)/shard_map/ppermute | solution.py:682
  147.1 6.2 %collective-permute-start.11 = (bf16[64,512]{1,0:T(8,128)(2,1)S(1)}, bf16[64,512]{1,0:T(8,128)(2,1)S(1)}, u32[]{:S(2)}, u32[]{:S(2)}) collective-permute-start(bf16[64,512]{1,0:T(8,128)(2,1)S(1)} %get-tuple-element.106.refs_2_.refs_0_), channel_id=1, source_target_pairs={{0,6},{1,7},{2,4},{3,5},{4,2},{5,3},{6,0},{7,1},{8,14},{9,15},{10,... | collective-permute-start | bytes 196616 | tf_op jit(solution)/shard_map/ppermute | solution.py:682
  153.3 8.7 %collective-permute-start.13 = (bf16[256,512]{1,0:T(8,128)(2,1)S(1)}, bf16[256,512]{1,0:T(8,128)(2,1)S(1)}, u32[]{:S(2)}, u32[]{:S(2)}) collective-permute-start(bf16[256,512]{1,0:T(8,128)(2,1)S(1)} %gather.1.refs_6_.refs_1_), channel_id=1, source_target_pairs={{0,1},{1,0},{2,3},{3,2},{4,5},{5,4},{6,7},{7,6},{8,9},{9,8},{10,11... | collective-permute-start | bytes 786440 | tf_op jit(solution)/shard_map/ppermute | solution.py:682
  154.8 8.7 %collective-permute-start.14 = (bf16[256,512]{1,0:T(8,128)(2,1)S(1)}, bf16[256,512]{1,0:T(8,128)(2,1)S(1)}, u32[]{:S(2)}, u32[]{:S(2)}) collective-permute-start(bf16[256,512]{1,0:T(8,128)(2,1)S(1)} %gather.1.refs_6_.refs_1_), channel_id=1, source_target_pairs={{0,16},{8,24},{16,0},{24,8},{1,17},{9,25},{17,1},{25,9},{2,18},{10... | collective-permute-start | bytes 786440 | tf_op jit(solution)/shard_map/ppermute | solution.py:680
  155.4 11.0 %collective-permute-start.15 = (bf16[256,512]{1,0:T(8,128)(2,1)S(1)}, bf16[256,512]{1,0:T(8,128)(2,1)S(1)}, u32[]{:S(2)}, u32[]{:S(2)}) collective-permute-start(bf16[256,512]{1,0:T(8,128)(2,1)S(1)} %gather.1.refs_6_.refs_1_), channel_id=1, source_target_pairs={{0,17},{1,16},{2,19},{3,18},{4,21},{5,20},{6,23},{7,22},{8,25},{9,... | collective-permute-start | bytes 786440 | tf_op jit(solution)/shard_map/ppermute | solution.py:686
  156.9 9.6 %collective-permute-start.16 = (bf16[256,512]{1,0:T(8,128)(2,1)S(1)}, bf16[256,512]{1,0:T(8,128)(2,1)S(1)}, u32[]{:S(2)}, u32[]{:S(2)}) collective-permute-start(bf16[256,512]{1,0:T(8,128)(2,1)S(1)} %gather.1.refs_6_.refs_1_), channel_id=1, source_target_pairs={{0,8},{8,0},{16,24},{24,16},{1,9},{9,1},{17,25},{25,17},{2,10},{10... | collective-permute-start | bytes 786440 | tf_op jit(solution)/shard_map/ppermute | solution.py:680
  162.0 4.4 %collective-permute-start.17 = (bf16[256,512]{1,0:T(8,128)(2,1)S(1)}, bf16[256,512]{1,0:T(8,128)(2,1)S(1)}, u32[]{:S(2)}, u32[]{:S(2)}) collective-permute-start(bf16[256,512]{1,0:T(8,128)(2,1)S(1)} %collective-permute-done.13.refs_2_), channel_id=1, source_target_pairs={{0,8},{8,0},{16,24},{24,16},{1,9},{9,1},{17,25},{25,17},{2,10},{10... | collective-permute-start | bytes 786440 | tf_op jit(solution)/shard_map/ppermute | solution.py:680
  163.6 2.9 %collective-permute-start.18 = (bf16[256,512]{1,0:T(8,128)(2,1)S(1)}, bf16[256,512]{1,0:T(8,128)(2,1)S(1)}, u32[]{:S(2)}, u32[]{:S(2)}) collective-permute-start(bf16[256,512]{1,0:T(8,128)(2,1)S(1)} %collective-permute-done.14.refs_3_), channel_id=1, source_target_pairs={{0,8},{8,0},{16,24},{24,16},{1,9},{9,1},{17,25},{25,17},{2,10},{10... | collective-permute-start | bytes 786440 | tf_op jit(solution)/shard_map/ppermute | solution.py:680
  166.4 1.5 collective-permute-start.19
  (3 other events, 53.1 us)
